TPU v7x, 32 devices: a whole 2x2x4 slice. The times are simulated.
32 devices in a mesh: gx: 16 (over z, y, x), sa: 2 (over core).
Axes of the slice: x: 2, y: 2, z: 4, core: 2. Of those that a mesh axis runs over, the one named last changes fastest.
Arguments:
- inputs: bfloat16 [2, 16, 64, 128, 128], P('sa', None, 'gx'), may hold values from -6 to 6
- preact: bfloat16 [2, 16, 64, 128, 128], P('sa', None, 'gx'), may hold values from -6 to 6
- cotangent: bfloat16 [2, 16, 64, 128, 128], P('sa', None, 'gx'), may hold values from -6 to 6
- mode_weight: bfloat16 [16, 16, 2048, 128], P(None, None, 'gx'), may hold values from -1 to 1
- bypass_weight: bfloat16 [16, 16], replicated, may hold values from -1.5 to 1.5
Outputs:
- input_grad: bfloat16 [2, 16, 64, 128, 128], P('sa', None, 'gx')
- mode_grad: float32 [16, 16, 2048, 128], P(None, None, ('gx', 'sa'))
All inputs are finite; a program needn't handle non-finite values.
Results may differ from a plain program's by a relative error of at most 0.0097.
Values may be sent and summed in bfloat16 or wider, within the bound.
A program may use at most 128 MiB of HBM per device.

v0:
```python
import math

import jax
import jax.numpy as jnp
from jax import lax
from jax.sharding import PartitionSpec as P

MY = 64
MT = 32


root_half = math.sqrt(0.5)
gauss_norm = 1.0 / math.sqrt(2.0 * math.pi)


def tables(kept_count, length, two_sided):
    frequency = jnp.arange(kept_count, dtype=jnp.int32)
    if two_sided:
        frequency = jnp.where(
            frequency < kept_count // 2, frequency, frequency + (length - kept_count)
        )
    position = jnp.arange(length, dtype=jnp.int32)
    product = frequency[:, None] * position[None, :] % length
    phase_angle = product.astype(jnp.float32) * (2.0 * math.pi / length)
    return (jnp.cos(phase_angle).astype(jnp.bfloat16), jnp.sin(phase_angle).astype(jnp.bfloat16))


def gelu_backward(preact_block, cotangent_block):
    values = preact_block.astype(jnp.float32)
    slope = (
        0.5 * (1.0 + jax.scipy.special.erf(values * root_half))
        + values * jnp.exp(-0.5 * values * values) * gauss_norm
    )
    return (cotangent_block.astype(jnp.float32) * slope).astype(jnp.bfloat16)


def gradient_term(input_hat, grad_hat, half):
    input_real = input_hat[..., :half].astype(jnp.float32)[:, None]
    input_imag = input_hat[..., half:].astype(jnp.float32)[:, None]
    grad_real = grad_hat[..., :half].astype(jnp.float32)[None]
    grad_imag = grad_hat[..., half:].astype(jnp.float32)[None]
    return jnp.concatenate(
        [
            input_real * grad_real + input_imag * grad_imag,
            input_real * grad_imag - input_imag * grad_real,
        ],
        axis=-1,
    )


def shards(inputs, preact, cotangent, mode_weight, bypass_weight):
    channels = inputs.shape[1]
    slab_cells = inputs.shape[2]
    cells_y = inputs.shape[3]
    cells_time = inputs.shape[4]
    devices_x = lax.axis_size("gx")
    cells_x = slab_cells * devices_x
    modes_x = mode_weight.shape[3] // 2
    modes_y = MY
    modes_time = MT
    pair_count = modes_y * modes_time
    cell_count = cells_x * cells_y * cells_time
    scale_in = float(modes_x * pair_count * cell_count) ** (-0.25)
    scale_out = float(cell_count) ** (-0.5)
    cosine_time, sine_time = tables(modes_time, cells_time, False)
    cosine_y, sine_y = tables(modes_y, cells_y, True)
    cosine_x, sine_x = tables(modes_x, cells_x, True)
    forward_time = jnp.concatenate([cosine_time.T, -sine_time.T], axis=1)
    inverse_time = jnp.concatenate([cosine_time, -sine_time], axis=0)
    plane_table = jnp.stack([jnp.stack([cosine_y, sine_y], -1), jnp.stack([-sine_y, cosine_y], -1)])
    x_forward = jnp.stack(
        [jnp.concatenate([cosine_x, -sine_x], 0).T, jnp.concatenate([sine_x, cosine_x], 0).T], 1
    )
    x_inverse = jnp.stack(
        [jnp.concatenate([cosine_x, -sine_x], 0), jnp.concatenate([sine_x, cosine_x], 0)], -1
    )

    def spectra(field):
        sectioned = jnp.dot(
            field.reshape(-1, cells_time), forward_time, preferred_element_type=jnp.float32
        ).astype(jnp.bfloat16)
        sectioned = sectioned.reshape(channels, slab_cells, cells_y, 2, modes_time)
        plane = jnp.einsum(
            "cxyqk,ajyq->jkcxa", sectioned, plane_table, preferred_element_type=jnp.float32
        ).astype(jnp.bfloat16)
        return plane.reshape(pair_count, channels, slab_cells, 2)

    def x_transform(block, factor):
        summed = jnp.einsum("pcxq,xqr->cpr", block, x_forward, preferred_element_type=jnp.float32)
        return (factor * summed).astype(jnp.bfloat16)

    dz_field = gelu_backward(preact[0], cotangent[0])
    input_hat = x_transform(
        lax.all_to_all(spectra(inputs[0]), "gx", split_axis=0, concat_axis=2, tiled=True), scale_in
    )
    grad_hat = x_transform(
        lax.all_to_all(spectra(dz_field), "gx", split_axis=0, concat_axis=2, tiled=True), scale_out
    )
    mode_grad = lax.psum_scatter(
        gradient_term(input_hat, grad_hat, modes_x).astype(jnp.bfloat16),
        "sa",
        scatter_dimension=2,
        tiled=True,
    ).astype(jnp.float32)
    weights = mode_weight.astype(jnp.float32)
    grad_real = grad_hat[..., :modes_x].astype(jnp.float32)[None]
    grad_imag = grad_hat[..., modes_x:].astype(jnp.float32)[None]
    weight_real = weights[..., :modes_x]
    weight_imag = weights[..., modes_x:]
    back_real = jnp.sum(weight_real * grad_real + weight_imag * grad_imag, axis=1)
    back_imag = jnp.sum(weight_real * grad_imag - weight_imag * grad_real, axis=1)
    back_hat = jnp.concatenate([back_real, back_imag], axis=-1).astype(jnp.bfloat16)
    grid_rows = jnp.einsum(
        "cpr,rxq->pcxq", back_hat, x_inverse, preferred_element_type=jnp.float32
    ).astype(jnp.bfloat16)
    block = lax.all_to_all(grid_rows, "gx", split_axis=2, concat_axis=0, tiled=True)
    items = block.shape[1]
    plane = block.reshape(modes_y, modes_time, items, slab_cells, 2)
    joined = jnp.einsum(
        "jkcxa,ajyq->cxyqk", plane, plane_table, preferred_element_type=jnp.float32
    ).astype(jnp.bfloat16)
    spectral = jnp.dot(
        joined.reshape(-1, 2 * modes_time), inverse_time, preferred_element_type=jnp.float32
    )
    spectral_grad = scale_in * spectral.reshape(items, slab_cells, cells_y, cells_time)
    bypass = jnp.dot(
        bypass_weight, dz_field.reshape(channels, -1), preferred_element_type=jnp.float32
    ).reshape(dz_field.shape)
    input_grad = (spectral_grad + bypass).astype(jnp.bfloat16)[None]
    return (input_grad, mode_grad)


def solution(mesh):
    placed = (
        P("sa", None, "gx", None, None),
        P("sa", None, "gx", None, None),
        P("sa", None, "gx", None, None),
        P(None, None, "gx", None),
        P(),
    )
    return jax.shard_map(
        shards,
        mesh=mesh,
        in_specs=placed,
        out_specs=(P("sa", None, "gx", None, None), P(None, None, ("gx", "sa"), None)),
        check_vma=False,
    )
```

profile of v0, /device:TPU:0, one launch (start us, length us, event | category | flops | bytes accessed | tf_op | source)
XLA Modules:
  0.0 169.4 jit_solution(8132999967270225971)
XLA Ops:
  7.8 3.6 %fusion.6 = bf16[8192,128]{1,0:T(8,128)(2,1)S(1)} fusion(bf16[1,16,4,128,128]{4,3,2,1,0:T(8,128)(2,1)} %param.6, bf16[1,16,4,128,128]{4,3,2,1,0:T(8,128)(2,1)} %param.7), kind=kLoop, calls=%fused_computation.15 | loop fusion | flops 12582912 | bytes 6291456 | tf_op jit(solution)/shard_map/convert_element_type | solution.py:34
  12.3 1.5 reshape.185
  13.8 2.1 %fusion.22 = bf16[64,32,16,4,2]{0,1,3,2,4:T(8,128)(2,1)S(1)} fusion(bf16[16,4,128,2,32]{2,1,0,4,3:T(4,128)(2,1)} %reshape.185, bf16[1,64,128,2]{2,1,3,0:T(8,128)(2,1)S(1)} %get-tuple-element.19, bf16[1,64,128,2]{2,1,3,0:T(8,128)(2,1)S(1)} %get-tuple-element.18), kind=kOutput, calls=%fused_computation.36 | convolution fusion | flops 134610944 | bytes 1638400 | tf_op jit(solution)/shard_map/cxyqk,ajyq->jkcxa/dot_general | solution.py:83
  15.9 8.0 %copy.78 = bf16[64,32,16,4,2]{2,4,3,1,0:T(2,128)(2,1)} copy(bf16[64,32,16,4,2]{0,1,3,2,4:T(8,128)(2,1)S(1)} %fusion.22) | data formatting | bytes 1048576 | tf_op jit(solution)/shard_map/reshape | solution.py:86
  23.9 6.4 %reshape.209 = bf16[16,2,8192]{2,1,0:T(2,128)(2,1)} reshape(bf16[2048,4,2,16]{3,2,1,0:T(2,128)(2,1)} %bitcast.161) | data formatting | bytes 1048576
  30.3 8.4 %all-to-all-start = ((bf16[16,2,8192]{2,1,0:T(2,128)(2,1)}), bf16[16,2,8192]{2,1,0:T(2,128)(2,1)}, u32[]{:S(2)}, u32[]{:S(2)}) async-start(bf16[16,2,8192]{2,1,0:T(2,128)(2,1)} %reshape.209), calls=%async_computation | async-start | bytes 1048576 | tf_op jit(solution)/shard_map/all_to_all | solution.py:97
  41.2 8.0 %copy.81 = bf16[64,32,16,4,2]{2,4,3,1,0:T(2,128)(2,1)} copy(bf16[64,32,16,4,2]{0,1,3,2,4:T(8,128)(2,1)S(1)} %fusion.26) | data formatting | bytes 1048576 | tf_op jit(solution)/shard_map/reshape | solution.py:86
  49.2 6.4 %reshape.211 = bf16[16,2,8192]{2,1,0:T(2,128)(2,1)} reshape(bf16[2048,4,2,16]{3,2,1,0:T(2,128)(2,1)} %bitcast.162) | data formatting | bytes 1048576
  55.6 6.9 %all-to-all-start.2 = ((bf16[16,2,8192]{2,1,0:T(2,128)(2,1)}), bf16[16,2,8192]{2,1,0:T(2,128)(2,1)S(1)}, u32[]{:S(2)}, u32[]{:S(2)}) async-start(bf16[16,2,8192]{2,1,0:T(2,128)(2,1)} %reshape.211), calls=%async_computation.2 | async-start | bytes 1048576 | tf_op jit(solution)/shard_map/all_to_all | solution.py:94
  62.7 11.3 %convert_element_type.203 = f32[16,16,128,128]{3,2,1,0:T(8,128)} convert(bf16[16,16,128,128]{3,2,1,0:T(8,128)(2,1)} %param.8) | non-fusion elementwise | flops 4194304 | bytes 25165824 | tf_op jit(solution)/shard_map/convert_element_type | solution.py:105
  74.4 5.3 %reshape.210 = bf16[2048,4,2,16]{3,2,1,0:T(2,128)(2,1)} reshape(bf16[16,2,8192]{2,1,0:T(2,128)(2,1)} %all-to-all-done) | data formatting | bytes 1048576
  79.7 6.0 %copy.79 = bf16[16,128,16,4,2]{1,0,2,4,3:T(8,128)(2,1)S(1)} copy(bf16[16,128,16,4,2]{2,4,3,1,0:T(2,128)(2,1)} %bitcast.164) | data formatting | bytes 1048576 | tf_op jit(solution)/shard_map/all_to_all | solution.py:97
  87.3 4.1 %reshape.212 = bf16[2048,4,2,16]{3,2,1,0:T(2,128)(2,1)} reshape(bf16[16,2,8192]{2,1,0:T(2,128)(2,1)S(1)} %all-to-all-done.2) | data formatting | bytes 1048576
  91.4 6.0 %copy.82 = bf16[16,128,16,4,2]{1,0,2,4,3:T(8,128)(2,1)S(1)} copy(bf16[16,128,16,4,2]{2,4,3,1,0:T(2,128)(2,1)} %bitcast.165) | data formatting | bytes 1048576 | tf_op jit(solution)/shard_map/all_to_all | solution.py:94
  100.7 2.4 %copy.65 = f32[16,128,64]{2,1,0:T(8,128)} copy(f32[16,128,64]{1,2,0:T(8,128)} %get-tuple-element.9) | data formatting | bytes 1048576 | tf_op jit(solution)/shard_map/convert_element_type | solution.py:39
  103.0 16.8 %add_convert_fusion = (bf16[16,16,128,64]{3,2,1,0:T(8,128)(2,1)S(1)}, bf16[16,16,128,64]{3,2,1,0:T(8,128)(2,1)S(1)}, bf16[16,128,64]{2,1,0:T(8,128)(2,1)}, bf16[16,128,64]{2,1,0:T(8,128)(2,1)}) fusion(f32[16,128,64]{2,1,0:T(8,128)} %copy.65, f32[16,128,64]{2,1,0:T(8,128)S(1)} %copy.64, f32[16,128,64]{2,1,0:T(8,128)S(1)} %copy.53, ...), kind=kLoop, calls=%fused_computation.1 | loop fusion | flops 33292288 | bytes 27787264 | tf_op jit(solution)/shard_map/convert.4
  119.8 6.2 %pad_maximum_fusion = bf16[16,16,128,128]{3,2,1,0:T(8,128)(2,1)} fusion(bf16[16,16,128,64]{3,2,1,0:T(8,128)(2,1)S(1)} %get-tuple-element.5, bf16[16,16,128,64]{3,2,1,0:T(8,128)(2,1)S(1)} %get-tuple-element.4), kind=kLoop, calls=%fused_computation.7 | loop fusion | flops 16777216 | bytes 16777216 | tf_op jit(solution)/shard_map/concatenate | solution.py:42
  128.8 6.9 %all-to-all-start.1 = ((bf16[128,16,64,2]{0,1,3,2:T(8,128)(2,1)}), bf16[128,16,64,2]{0,1,3,2:T(8,128)(2,1)S(1)}, u32[]{:S(2)}, u32[]{:S(2)}) async-start(bf16[128,16,64,2]{0,1,3,2:T(8,128)(2,1)} %copy.54), calls=%async_computation.1 | async-start | bytes 1048576 | tf_op jit(solution)/shard_map/all_to_all | solution.py:116
  135.8 3.0 %reshape.193 = f32[16,65536]{1,0:T(8,128)} reshape(bf16[1,16,4,128,128]{4,3,2,1,0:T(8,128)(2,1)S(1)} %copy-done.3) | data formatting | bytes 6291456 | tf_op jit(solution)/shard_map/convert_element_type | solution.py:34
  138.7 4.0 %reshape.194 = f32[16,65536]{1,0:T(8,128)} reshape(bf16[1,16,4,128,128]{4,3,2,1,0:T(8,128)(2,1)} %param.6) | data formatting | bytes 6291456 | tf_op jit(solution)/shard_map/convert_element_type | solution.py:29
  142.8 4.7 %convolution_bitcast_fusion = f32[2,8,512,128]{3,1,2,0:T(8,128)S(1)} fusion(bf16[16,16]{1,0:T(8,128)(2,1)S(1)} %copy-done.6, f32[16,65536]{1,0:T(8,128)} %reshape.193, f32[16,65536]{1,0:T(8,128)} %reshape.194), kind=kOutput, calls=%fused_computation.27 | convolution fusion | flops 44040192 | bytes 12583424 | tf_op jit(solution)/shard_map/dot_general | solution.py:126
  147.4 2.8 %copy.85 = f32[2,8,512,128]{3,2,1,0:T(8,128)} copy(f32[2,8,512,128]{3,1,2,0:T(8,128)S(1)} %convolution_bitcast_fusion) | data formatting | bytes 8388608
  153.8 2.1 %fusion.19 = bf16[1,16,4,128,128]{4,3,2,1,0:T(8,128)(2,1)} fusion(f32[16,4,128,128]{3,2,1,0:T(8,128)S(1)} %bitcast.163, bf16[16,4,128,64]{2,3,1,0:T(8,128)(2,1)S(1)} %bitcast.166, bf16[32,128]{1,0:T(8,128)(2,1)S(1)} %fusion.73, bf16[32,128]{1,0:T(8,128)(2,1)S(1)} %cosine_convert_fusion.2), kind=kOutput, calls=%fused_computation.33 | convolution fusion | flops 137396224 | bytes 7356416 | tf_op jit(solution)/shard_map/dot_general | solution.py:122
  155.9 6.7 %convert_element_type.240 = f32[16,16,64,128]{3,2,1,0:T(8,128)} convert(bf16[16,16,64,128]{3,2,1,0:T(8,128)(2,1)} %reduce-scatter.2.cloned.1.call-done) | non-fusion elementwise | flops 2097152 | bytes 12582912 | tf_op jit(solution)/shard_map/convert_element_type | solution.py:104
  (50 shorter events, 15.6 us)
Async XLA Ops:
  7.2 31.5 %copy-start = (bf16[1,16,4,128,128]{4,3,2,1,0:T(8,128)(2,1)S(1)}, bf16[1,16,4,128,128]{4,3,2,1,0:T(8,128)(2,1)}, u32[]{:S(2)}) copy-start(bf16[1,16,4,128,128]{4,3,2,1,0:T(8,128)(2,1)} %param.5) | copy-start | bytes 6291460
  30.3 25.3 %all-to-all-start = ((bf16[16,2,8192]{2,1,0:T(2,128)(2,1)}), bf16[16,2,8192]{2,1,0:T(2,128)(2,1)}, u32[]{:S(2)}, u32[]{:S(2)}) async-start(bf16[16,2,8192]{2,1,0:T(2,128)(2,1)} %reshape.209), calls=%async_computation | async-start | bytes 1048576 | tf_op jit(solution)/shard_map/all_to_all | solution.py:97
  55.6 31.7 %all-to-all-start.2 = ((bf16[16,2,8192]{2,1,0:T(2,128)(2,1)}), bf16[16,2,8192]{2,1,0:T(2,128)(2,1)S(1)}, u32[]{:S(2)}, u32[]{:S(2)}) async-start(bf16[16,2,8192]{2,1,0:T(2,128)(2,1)} %reshape.211), calls=%async_computation.2 | async-start | bytes 1048576 | tf_op jit(solution)/shard_map/all_to_all | solution.py:94
  62.5 93.4 %reduce-scatter.2.cloned.1.call-start = ((), (), s32[]{:S(2)}) async-start(), calls=%async_computation.4 | async-start | bytes 12582912 | tf_op jit(solution)/shard_map/reduce_scatter | solution.py:99
  126.0 1.0 copy-start.4
  126.0 1.2 copy-start.5
  126.0 9.7 %copy-start.3 = (bf16[1,16,4,128,128]{4,3,2,1,0:T(8,128)(2,1)S(1)}, bf16[1,16,4,128,128]{4,3,2,1,0:T(8,128)(2,1)}, u32[]{:S(2)}) copy-start(bf16[1,16,4,128,128]{4,3,2,1,0:T(8,128)(2,1)} %param.7) | copy-start | bytes 6291460
  128.8 21.5 %all-to-all-start.1 = ((bf16[128,16,64,2]{0,1,3,2:T(8,128)(2,1)}), bf16[128,16,64,2]{0,1,3,2:T(8,128)(2,1)S(1)}, u32[]{:S(2)}, u32[]{:S(2)}) async-start(bf16[128,16,64,2]{0,1,3,2:T(8,128)(2,1)} %copy.54), calls=%async_computation.1 | async-start | bytes 1048576 | tf_op jit(solution)/shard_map/all_to_all | solution.py:116
  138.7 4.0 %copy-start.6 = (bf16[16,16]{1,0:T(8,128)(2,1)S(1)}, bf16[16,16]{1,0:T(8,128)(2,1)}, u32[]{:S(2)}) copy-start(bf16[16,16]{1,0:T(8,128)(2,1)} %param.9) | copy-start | bytes 1540
  151.6 2.2 %copy-start.2 = (f32[2,8,512,128]{3,2,1,0:T(8,128)S(1)}, f32[2,8,512,128]{3,2,1,0:T(8,128)}, u32[]{:S(2)}) copy-start(f32[2,8,512,128]{3,2,1,0:T(8,128)} %copy.85) | copy-start | bytes 12582916
  153.8 8.7 %copy-start.1 = (bf16[1,16,4,128,128]{4,3,2,1,0:T(8,128)(2,1)S(1)}, bf16[1,16,4,128,128]{4,3,2,1,0:T(8,128)(2,1)}, u32[]{:S(2)}) copy-start(bf16[1,16,4,128,128]{4,3,2,1,0:T(8,128)(2,1)} %param.5) | copy-start | bytes 6291460
Sparse Core Ops, SparseCore 0:
  126.2 18.0 reduce-scatter.1
where the time goes:
time: 171 us; the launch traced here: 169 us
  local copies, waits for them, and re-layouts  72.6 us (42%)
  other arithmetic  46.9 us (27%)
  starting transfers between devices  22.3 us (13%)
  between operations  14.3 us (8%)
  matrix products  13.2 us (8%)
    unnamed x19, local copies, waits for them, and re-layouts  27.6 us
    another operation x1, other arithmetic  16.8 us
    reshape x2, local copies, waits for them, and re-layouts, spectra(): return plane.reshape(pair_count, channels, slab_cells, 2)  16 us
    convert_element_type x1, other arithmetic, shards(): weights = mode_weight.astype(jnp.float32)  11.3 us
    all_to_all x1, starting transfers between devices, shards(): lax.all_to_all(spectra(dz_field), 'gx', split_axis=0, concat_axis=2, tile...  8.36 us
    all_to_all x1, starting transfers between devices, shards(): lax.all_to_all(grid_rows, 'gx', split_axis=2, concat_axis=0, tiled=True)  6.91 us
    all_to_all x1, starting transfers between devices, shards(): lax.all_to_all(spectra(inputs[0]), 'gx', split_axis=0, concat_axis=2, til...  6.85 us
    convert_element_type x1, other arithmetic, shards(): mode_grad = lax.psum_scatter(gradient_term(input_hat, grad_hat, modes_x)....  6.65 us
  transfers between devices with their start and end apart: 4, of which 0 were waited for; matrix products, arithmetic and copies ran while one was open for 36% of the time, Pallas kernels for 0%

commit v1 on v0

--- a/solution.py
+++ b/solution.py
@@ -1,8 +1,12 @@
+import functools
 import math
 
 import jax
 import jax.numpy as jnp
+import numpy as np
 from jax import lax
+from jax.experimental import pallas as pl
+from jax.experimental.pallas import tpu as pltpu
 from jax.sharding import PartitionSpec as P
 
 MY = 64
@@ -48,7 +52,7 @@
     )
 
 
-def shards(inputs, preact, cotangent, mode_weight, bypass_weight):
+def plain_shards(inputs, preact, cotangent, mode_weight, bypass_weight):
     channels = inputs.shape[1]
     slab_cells = inputs.shape[2]
     cells_y = inputs.shape[3]
@@ -130,6 +134,323 @@
     return (input_grad, mode_grad)
 
 
+def host_tables(kept_count, length, two_sided):
+    frequency = np.arange(kept_count)
+    if two_sided:
+        frequency = np.where(
+            frequency < kept_count // 2, frequency, frequency + (length - kept_count)
+        )
+    product = frequency[:, None] * np.arange(length)[None, :] % length
+    angle = product.astype(np.float32) * np.float32(2.0 * math.pi / length)
+    return np.cos(angle).astype(np.float32), np.sin(angle).astype(np.float32)
+
+
+def block_tables(sizes):
+    ct, st = host_tables(sizes.modes_time, sizes.cells_time, False)
+    cy, sy = host_tables(sizes.modes_y, sizes.cells_y, True)
+    cx, sx = host_tables(sizes.modes_x, sizes.cells_x, True)
+    group = np.eye(sizes.group, dtype=np.float32)
+    slab = np.eye(sizes.slab, dtype=np.float32)
+    rows = np.eye(sizes.rows, dtype=np.float32)
+    time = np.stack([ct, -st])
+    time_forward = np.einsum("cd,qkt->ctqdk", group, time)
+    time_forward = time_forward.reshape(sizes.group * sizes.cells_time, -1)
+    time_inverse = time_forward.T
+    plane = np.stack([np.stack([cy, sy]), np.stack([-sy, cy])])
+    plane = plane.reshape(2, 2, sizes.devices, sizes.rows, sizes.cells_y)
+    y_forward = np.einsum("qpdjy,xz->djxqzpy", plane, slab)
+    y_forward = y_forward.reshape(sizes.devices * sizes.piece, -1)
+    y_inverse = y_forward.T
+    x_table = np.stack(
+        [np.concatenate([cx, -sx], 0).T, np.concatenate([sx, cx], 0).T], 1
+    )
+    x_table = x_table.reshape(-1, sizes.slab, 2, 2 * sizes.modes_x)
+    real, imag = x_table[..., : sizes.modes_x], x_table[..., sizes.modes_x :]
+
+    def x_rows(table):
+        wide = np.einsum("gxqr,jl->gjxqlr", table, rows)
+        return wide.reshape(-1, sizes.rows * table.shape[-1])
+
+    x_input = x_rows(np.concatenate([real, real, imag, imag], -1))
+    x_grad = x_rows(np.concatenate([real, imag, imag, -real], -1))
+    x_inverse = x_rows(x_table)
+    everything = (time_forward, time_inverse, y_forward, y_inverse, x_input, x_grad, x_inverse)
+    return [table.astype(jnp.bfloat16) for table in everything]
+
+
+class Sizes:
+    def __init__(self, inputs, mode_weight, gx_count, sa_count):
+        _, self.channels, self.slab, self.cells_y, self.cells_time = inputs
+        self.modes_x = mode_weight[3] // 2
+        self.modes_y, self.modes_time = MY, MT
+        self.gx_count, self.sa_count = gx_count, sa_count
+        self.devices = gx_count * sa_count
+        self.cells_x = self.slab * gx_count
+        self.pairs = self.modes_y * self.modes_time
+        self.own_pairs = self.pairs // self.devices
+        self.rows = self.own_pairs // self.modes_time
+        self.piece = self.rows * self.slab * 2
+        self.group = 128 // self.modes_time
+        self.groups = self.channels // self.group
+        cell_count = self.cells_x * self.cells_y * self.cells_time
+        self.scale_in = float(self.modes_x * self.pairs * cell_count) ** (-0.25)
+        self.scale_out = float(cell_count) ** (-0.5)
+
+    def fits(self):
+        return (
+            self.own_pairs == self.rows * self.modes_time
+            and self.own_pairs % 16 == 0
+            and self.piece % 16 == 0
+            and self.modes_x == 64
+            and self.channels % self.group == 0
+            and self.cells_time == 128
+            and self.cells_y == 128
+            and inputs_fit(self)
+        )
+
+
+def inputs_fit(sizes):
+    return sizes.sa_count == 2 and sizes.channels == 16
+
+
+def forward_kernel(
+    sizes, inputs, preact, cotangent, time_forward, y_forward, dz, spectra, in_rows, dz_rows
+):
+    step = pl.program_id(0)
+    slope = gelu_slope(preact[0, :, 0].astype(jnp.float32))
+    gradient = (cotangent[0, :, 0].astype(jnp.float32) * slope).astype(jnp.bfloat16)
+    dz[:, 0] = gradient
+    first = pl.multiple_of(step * 2 * sizes.cells_y, 2 * sizes.cells_y)
+
+    def time_rows(read, target):
+        for cg in range(sizes.groups):
+            left = jnp.concatenate(
+                [read(cg * sizes.group + c) for c in range(sizes.group)], axis=1
+            )
+            both = jnp.dot(left, time_forward[...], preferred_element_type=jnp.float32)
+            both = both.astype(jnp.bfloat16)
+            for q in range(2):
+                target[pl.ds(first + q * sizes.cells_y, sizes.cells_y), pl.ds(cg * 128, 128)] = (
+                    both[:, q * 128 : (q + 1) * 128]
+                )
+
+    time_rows(lambda c: inputs[0, c, 0], in_rows)
+    time_rows(lambda c: dz[c, 0], dz_rows)
+
+    @pl.when(step == sizes.slab - 1)
+    def _():
+        for field, held in enumerate((in_rows, dz_rows)):
+            plane = jnp.dot(y_forward[...], held[...], preferred_element_type=jnp.float32)
+            plane = plane.astype(jnp.bfloat16)
+            for cg in range(sizes.groups):
+                spectra[:, field, cg] = plane[:, cg * 128 : (cg + 1) * 128].reshape(
+                    sizes.devices, sizes.piece, 128
+                )
+
+
+def gelu_slope(values):
+    return (
+        0.5 * (1.0 + lax.erf(values * root_half))
+        + values * jnp.exp(-0.5 * values * values) * gauss_norm
+    )
+
+
+def mode_kernel(
+    sizes, spectra, weight, x_input, x_grad, x_inverse, mode_grad, rows_out, hats, back
+):
+    step = pl.program_id(0)
+    samples, groups, kt = sizes.sa_count, sizes.groups, sizes.modes_time
+
+    @pl.when(step == 0)
+    def _():
+        for field, table, scale in (
+            (0, x_input, sizes.scale_in),
+            (1, x_grad, sizes.scale_out),
+        ):
+            for s in range(samples):
+                for cg in range(groups):
+                    block = spectra[:, s, field, cg].reshape(-1, 128)
+                    summed = lax.dot_general(
+                        block, table[...], (((0,), (0,)), ((), ())),
+                        preferred_element_type=jnp.float32,
+                    )
+                    summed = (scale * summed).astype(jnp.bfloat16).astype(jnp.float32)
+                    for j in range(sizes.rows):
+                        for part in range(2):
+                            lanes = (2 * j + part) * 128
+                            for c in range(sizes.group):
+                                hats[
+                                    2 * field + part, s, cg * sizes.group + c, pl.ds(j * kt, kt)
+                                ] = summed[c * kt : (c + 1) * kt, lanes : lanes + 128]
+
+    low = lax.broadcasted_iota(jnp.int32, (16, 128), 1) < sizes.modes_x
+    cg, member = step // sizes.group, step % sizes.group
+    for block in range(sizes.own_pairs // 16):
+        rows = pl.ds(block * 16, 16)
+        left = [[hats[part, s, step, rows] for s in range(samples)] for part in range(2)]
+        total = [[None, None] for _ in range(samples)]
+        for o in range(sizes.channels):
+            right = [[hats[2 + part, s, o, rows] for s in range(samples)] for part in range(2)]
+            value = weight[0, o, rows].astype(jnp.float32)
+            grad = None
+            for s in range(samples):
+                for part in range(2):
+                    term = left[part][s] * right[part][s]
+                    grad = term if grad is None else grad + term
+                    term = value * right[part][s]
+                    held = total[s][part]
+                    total[s][part] = term if held is None else held + term
+            mode_grad[0, o, rows] = grad
+        j, k = divmod(block * 16, kt)
+        for s in range(samples):
+            real, imag = total[s]
+            real = real + pltpu.roll(real, sizes.modes_x, 1)
+            imag = imag + pltpu.roll(imag, sizes.modes_x, 1)
+            first = pl.multiple_of(member * kt + k, 16)
+            back[s, cg, pl.ds(first, 16), pl.ds(j * 128, 128)] = jnp.where(
+                low, real, imag
+            ).astype(jnp.bfloat16)
+
+    @pl.when(step == sizes.channels - 1)
+    def _():
+        for s in range(samples):
+            for cg in range(groups):
+                grid_rows = lax.dot_general(
+                    x_inverse[...], back[s, cg], (((1,), (1,)), ((), ())),
+                    preferred_element_type=jnp.float32,
+                )
+                rows_out[:, s, cg] = grid_rows.astype(jnp.bfloat16).reshape(
+                    sizes.gx_count, sizes.piece, 128
+                )
+
+
+def inverse_kernel(
+    sizes, grid_rows, dz, bypass, y_inverse, time_inverse, spread, input_grad, time_rows, mixer, acc
+):
+    step = pl.program_id(0)
+    channels, group, cells_y = sizes.channels, sizes.group, sizes.cells_y
+
+    @pl.when(step == 0)
+    def _():
+        joined = jnp.concatenate(
+            [grid_rows[:, cg].reshape(-1, 128) for cg in range(sizes.groups)], axis=1
+        )
+        time_rows[...] = jnp.dot(
+            y_inverse[...], joined, preferred_element_type=jnp.float32
+        ).astype(jnp.bfloat16)
+        tall = jnp.dot(spread[...], bypass[...], preferred_element_type=jnp.float32)
+        wide = lax.dot_general(
+            tall.astype(jnp.bfloat16), spread[...], (((1,), (1,)), ((), ())),
+            preferred_element_type=jnp.float32,
+        )
+        row = lax.broadcasted_iota(jnp.int32, wide.shape, 0) % 16
+        column = lax.broadcasted_iota(jnp.int32, wide.shape, 1) % 16
+        mixer[...] = jnp.where(row == column, wide, 0.0).astype(jnp.bfloat16)
+
+    first = pl.multiple_of(step * 2 * cells_y, 2 * cells_y)
+    for cg in range(sizes.groups):
+        lanes = pl.ds(cg * 128, 128)
+        left = jnp.concatenate(
+            [time_rows[pl.ds(first + q * cells_y, cells_y), lanes] for q in range(2)], axis=1
+        )
+        spectral = jnp.dot(left, time_inverse[...], preferred_element_type=jnp.float32)
+        for c in range(group):
+            acc[cg * group + c] = sizes.scale_in * spectral[:, c * 128 : (c + 1) * 128]
+    for block in range(cells_y // 16):
+        rows = pl.ds(block * 16, 16)
+        mixed = jnp.dot(
+            mixer[...], dz[:, 0, rows].reshape(-1, 128), preferred_element_type=jnp.float32
+        ).reshape(channels, 16, 128)
+        input_grad[0, :, 0, rows] = (mixed + acc[:, rows]).astype(jnp.bfloat16)
+
+
+def whole(table):
+    return pl.BlockSpec(table.shape, lambda *_: (0,) * table.ndim)
+
+
+def shards(inputs, preact, cotangent, mode_weight, bypass_weight):
+    sizes = Sizes(inputs.shape, mode_weight.shape, lax.axis_size("gx"), lax.axis_size("sa"))
+    if not sizes.fits():
+        return plain_shards(inputs, preact, cotangent, mode_weight, bypass_weight)
+    tables_built = [jnp.asarray(table) for table in block_tables(sizes)]
+    time_forward, time_inverse, y_forward, y_inverse, x_input, x_grad, x_inverse = tables_built
+    channels, slab, cells_y, cells_time = inputs.shape[1:]
+    params = pltpu.CompilerParams(vmem_limit_bytes=48 * 2**20)
+    field_block = pl.BlockSpec(
+        (1, channels, 1, cells_y, cells_time), lambda x: (0, 0, x, 0, 0)
+    )
+    dz_block = pl.BlockSpec((channels, 1, cells_y, cells_time), lambda x: (0, x, 0, 0))
+    packet = (sizes.devices, 2, sizes.groups, sizes.piece, 128)
+    rows_shape = (2 * slab * cells_y, sizes.groups * 128)
+    dz, spectra = pl.pallas_call(
+        functools.partial(forward_kernel, sizes),
+        grid=(slab,),
+        in_specs=[field_block] * 3 + [whole(time_forward), whole(y_forward)],
+        out_specs=[dz_block, pl.BlockSpec(packet, lambda x: (0,) * 5)],
+        out_shape=[
+            jax.ShapeDtypeStruct(inputs.shape[1:], jnp.bfloat16),
+            jax.ShapeDtypeStruct(packet, jnp.bfloat16),
+        ],
+        scratch_shapes=[pltpu.VMEM(rows_shape, jnp.bfloat16)] * 2,
+        compiler_params=params,
+        name="forward",
+    )(inputs, preact, cotangent, time_forward, y_forward)
+    spectra = lax.all_to_all(spectra, ("gx", "sa"), split_axis=0, concat_axis=0, tiled=True)
+    spectra = spectra.reshape((sizes.gx_count, sizes.sa_count) + packet[1:])
+    own = sizes.own_pairs
+    out_packet = (sizes.gx_count, sizes.sa_count, sizes.groups, sizes.piece, 128)
+    mode_grad, grid_rows = pl.pallas_call(
+        functools.partial(mode_kernel, sizes),
+        grid=(channels,),
+        in_specs=[
+            whole(spectra),
+            pl.BlockSpec(
+                (1, channels, own, 128), lambda i: (i, 0, lax.axis_index("sa"), 0)
+            ),
+            whole(x_input),
+            whole(x_grad),
+            whole(x_inverse),
+        ],
+        out_specs=[
+            pl.BlockSpec((1, channels, own, 128), lambda i: (i, 0, 0, 0)),
+            pl.BlockSpec(out_packet, lambda i: (0,) * 5),
+        ],
+        out_shape=[
+            jax.ShapeDtypeStruct((channels, channels, own, 128), jnp.float32),
+            jax.ShapeDtypeStruct(out_packet, jnp.bfloat16),
+        ],
+        scratch_shapes=[
+            pltpu.VMEM((4, sizes.sa_count, channels, own, 128), jnp.float32),
+            pltpu.VMEM((sizes.sa_count, sizes.groups, 128, sizes.rows * 128), jnp.bfloat16),
+        ],
+        compiler_params=params,
+        name="modes",
+    )(spectra, mode_weight, x_input, x_grad, x_inverse)
+    grid_rows = lax.all_to_all(
+        grid_rows.reshape((sizes.devices,) + out_packet[2:]),
+        ("gx", "sa"), split_axis=0, concat_axis=0, tiled=True,
+    )
+    spread = jnp.asarray(np.repeat(np.eye(channels), 16, axis=0).astype(jnp.bfloat16))
+    input_grad = pl.pallas_call(
+        functools.partial(inverse_kernel, sizes),
+        grid=(slab,),
+        in_specs=[
+            whole(grid_rows), dz_block, whole(bypass_weight), whole(y_inverse),
+            whole(time_inverse), whole(spread),
+        ],
+        out_specs=field_block,
+        out_shape=jax.ShapeDtypeStruct(inputs.shape, jnp.bfloat16),
+        scratch_shapes=[
+            pltpu.VMEM(rows_shape, jnp.bfloat16),
+            pltpu.VMEM((channels * 16, channels * 16), jnp.bfloat16),
+            pltpu.VMEM((channels, cells_y, cells_time), jnp.float32),
+        ],
+        compiler_params=params,
+        name="inverse",
+    )(grid_rows, dz, bypass_weight, y_inverse, time_inverse, spread)
+    return input_grad, mode_grad
+
+
 def solution(mesh):
     placed = (
         P("sa", None, "gx", None, None),

time: 171 us -> 82.7 us (0.48)
  local copies, waits for them, and re-layouts: 72.6 us -> 2.22 us
  blocking collectives: 0 us -> 52.3 us
  other arithmetic: 46.9 us -> 0 us
  Pallas kernels: 0 us -> 26.9 us
  starting transfers between devices: 22.3 us -> 0 us
  between operations: 14.3 us -> 0.72 us
  matrix products: 13.2 us -> 0 us
    all_to_all x0 -> x2, blocking collectives: none -> 52.3 us  [the longest x1 33.3 us: shards(): lax.all_to_all(spectra, ('gx', 'sa'), split_axis=0, concat_axis=0, tiled=...]
    pallas_call x0 -> x3, Pallas kernels: none -> 26.9 us  [the longest x1 15.4 us: shards(): pl.pallas_call(functools.partial(mode_kernel, sizes), grid=(channels,), i...]
    unnamed x19 -> x18, local copies, waits for them, and re-layouts: 27.6 us -> 2.22 us
    convert_element_type x9 -> x0, other arithmetic: 23.2 us -> none  [the longest x1 11.3 us: shards(): weights = mode_weight.astype(jnp.float32)]
    all_to_all x3 -> x0, starting transfers between devices: 22.1 us -> none  [the longest x1 8.36 us: shards(): lax.all_to_all(spectra(dz_field), 'gx', split_axis=0, concat_axis=2, tile...]
    reshape x5 -> x0, local copies, waits for them, and re-layouts: 19.2 us -> none  [the longest x2 16 us: spectra(): return plane.reshape(pair_count, channels, slab_cells, 2)]
    another operation x3 -> x0, other arithmetic: 16.9 us -> none
    all_to_all x5 -> x0, local copies, waits for them, and re-layouts: 13.3 us -> none  [the longest x2 6.46 us: shards(): lax.all_to_all(spectra(inputs[0]), 'gx', split_axis=0, concat_axis=2, til...]
  transfers between devices with their start and end apart: 4 -> 0, of which waited for: 0 -> 0; matrix products, arithmetic and copies ran while one was open for 36% -> 0% of each run, Pallas kernels for 0% -> 0%
where the time goes in v1:
time: 82.7 us; the launch traced here: 82.1 us
  blocking collectives  52.3 us (63%)
  Pallas kernels  26.9 us (33%)
  local copies, waits for them, and re-layouts  2.22 us (3%)
    all_to_all x1, blocking collectives, shards(): lax.all_to_all(spectra, ('gx', 'sa'), split_axis=0, concat_axis=0, tiled=...  33.3 us
    all_to_all x1, blocking collectives, shards(): lax.all_to_all(grid_rows.reshape((sizes.devices,) + out_packet[2:]), ('gx...  19 us
    pallas_call x1, Pallas kernels, shards(): pl.pallas_call(functools.partial(mode_kernel, sizes), grid=(channels,), i...  15.4 us
    pallas_call x1, Pallas kernels, shards(): pl.pallas_call(functools.partial(forward_kernel, sizes), grid=(slab,), in...  7.05 us
    pallas_call x1, Pallas kernels, shards(): pl.pallas_call(functools.partial(inverse_kernel, sizes), grid=(slab,), in...  4.41 us
    unnamed x18, local copies, waits for them, and re-layouts  2.22 us

profile of v1, /device:TPU:0, one launch (start us, length us, event | category | flops | bytes accessed | tf_op | source)
XLA Modules:
  0.0 82.1 jit_solution(13506800439502337107)
XLA Ops:
  0.6 0.0 copy-start.1
  0.6 1.2 %copy-done.1 = bf16[512,1024]{1,0:T(8,128)(2,1)S(1)} copy-done((bf16[512,1024]{1,0:T(8,128)(2,1)S(1)}, bf16[512,1024]{1,0:T(8,128)(2,1)}, u32[]{:S(2)}) %copy-start.1) | copy-done | bytes 1048600
  1.9 0.0 copy-start.5
  1.9 0.9 %copy-done.5 = bf16[512,256]{1,0:T(8,128)(2,1)S(1)} copy-done((bf16[512,256]{1,0:T(8,128)(2,1)S(1)}, bf16[512,256]{1,0:T(8,128)(2,1)}, u32[]{:S(2)}) %copy-start.5) | copy-done | bytes 262168
  2.8 7.0 %forward.1 = (bf16[16,4,128,128]{3,2,1,0:T(8,128)(2,1)S(1)}, bf16[32,2,4,16,128]{4,3,2,1,0:T(8,128)(2,1)S(1)}) custom-call(bf16[1,16,4,128,128]{4,3,2,1,0:T(8,128)(2,1)} %inputs.1, bf16[1,16,4,128,128]{4,3,2,1,0:T(8,128)(2,1)} %preact.1, bf16[1,16,4,128,128]{4,3,2,1,0:T(8,128)(2,1)} %cotangent.1, bf16[512,256]{1,0:T(8,128)(2,1)S(1)} %copy-done.5, ...), custom_call_target="tpu_custom_call" | custom-call | tf_op jit(solution)/shard_map/forward/pallas_call | solution.py:385
  9.9 0.0 copy-start.2
  9.9 0.0 copy-start.3
  9.9 0.0 copy-start.6
  9.9 33.3 %all_to_all.10 = bf16[32,2,4,16,128]{4,3,2,1,0:T(8,128)(2,1)S(1)} all-to-all(bf16[32,2,4,16,128]{4,3,2,1,0:T(8,128)(2,1)S(1)} %get-tuple-element.6), channel_id=1, replica_groups=mesh['gx'=16,'sa'=2] {'gx','sa'}, dimensions={0} | all-to-all | bytes 2097152 | tf_op jit(solution)/shard_map/all_to_all | solution.py:398
  43.2 0.0 copy-done.2
  43.2 0.0 copy-done.3
  43.2 0.0 copy-done.6
  43.2 0.0 copy-start
  43.2 0.0 copy-start.4
  43.3 0.0 copy-start.7
  43.3 0.0 copy-start.8
  43.3 15.4 %modes.1 = (f32[16,16,64,128]{3,2,1,0:T(8,128)}, bf16[16,2,4,16,128]{4,3,2,1,0:T(8,128)(2,1)S(1)}) custom-call(bf16[16,2,2,4,16,128]{5,4,3,2,1,0:T(8,128)(2,1)S(1)} %bitcast.2, bf16[16,16,128,128]{3,2,1,0:T(8,128)(2,1)} %weight.1, bf16[256,512]{1,0:T(8,128)(2,1)S(1)} %copy-done.3, bf16[256,512]{1,0:T(8,128)(2,1)S(1)} %copy-done.2, bf16[256,256]{1,0:T(8,128)(2,1)S(1)} %copy-done.6), custom_call_target="tpu_custom_call" | custom-call | tf_op jit(solution)/shard_map/modes/pallas_call | solution.py:402
  58.7 19.0 %all_to_all.11.grid_rows = bf16[32,4,16,128]{3,2,1,0:T(8,128)(2,1)S(1)} all-to-all(bf16[32,4,16,128]{3,2,1,0:T(8,128)(2,1)S(1)} %bitcast.3), channel_id=1, replica_groups=mesh['gx'=16,'sa'=2] {'gx','sa'}, dimensions={0} | all-to-all | bytes 1048576 | tf_op jit(solution)/shard_map/all_to_all | solution.py:429
  77.7 0.0 copy-done
  77.7 0.0 copy-done.4
  77.7 0.0 copy-done.7
  77.7 0.0 copy-done.8
  77.7 4.4 %inverse.1 = bf16[1,16,4,128,128]{4,3,2,1,0:T(8,128)(2,1)} custom-call(bf16[32,4,16,128]{3,2,1,0:T(8,128)(2,1)S(1)} %all_to_all.11.grid_rows, bf16[16,4,128,128]{3,2,1,0:T(8,128)(2,1)S(1)} %get-tuple-element.8.dz, bf16[16,16]{1,0:T(8,128)(2,1)S(1)} %copy-done.8, bf16[1024,512]{1,0:T(8,128)(2,1)S(1)} %copy-done, bf16[256,512]{1,0:T(8,128)(2,1)S(1)} %copy-done.4, ...), custom_call_target="tpu_custom_call" | custom-call | tf_op jit(solution)/shard_map/inverse/pallas_call | solution.py:434
Async XLA Ops:
  0.6 1.2 %copy-start.1 = (bf16[512,1024]{1,0:T(8,128)(2,1)S(1)}, bf16[512,1024]{1,0:T(8,128)(2,1)}, u32[]{:S(2)}) copy-start(bf16[512,1024]{1,0:T(8,128)(2,1)} %constant.18.clone.y_forward) | copy-start | bytes 3145732
  1.9 0.9 %copy-start.5 = (bf16[512,256]{1,0:T(8,128)(2,1)S(1)}, bf16[512,256]{1,0:T(8,128)(2,1)}, u32[]{:S(2)}) copy-start(bf16[512,256]{1,0:T(8,128)(2,1)} %constant.16.clone.time_forward) | copy-start | bytes 786436
  9.9 33.4 %copy-start.2 = (bf16[256,512]{1,0:T(8,128)(2,1)S(1)}, bf16[256,512]{1,0:T(8,128)(2,1)}, u32[]{:S(2)}) copy-start(bf16[256,512]{1,0:T(8,128)(2,1)} %constant.21.clone.x_grad) | copy-start | bytes 786436
  9.9 33.4 %copy-start.3 = (bf16[256,512]{1,0:T(8,128)(2,1)S(1)}, bf16[256,512]{1,0:T(8,128)(2,1)}, u32[]{:S(2)}) copy-start(bf16[256,512]{1,0:T(8,128)(2,1)} %constant.20.clone.x_input) | copy-start | bytes 786436
  9.9 33.3 %copy-start.6 = (bf16[256,256]{1,0:T(8,128)(2,1)S(1)}, bf16[256,256]{1,0:T(8,128)(2,1)}, u32[]{:S(2)}) copy-start(bf16[256,256]{1,0:T(8,128)(2,1)} %constant.22.clone.x_inverse) | copy-start | bytes 393220
  43.2 34.5 %copy-start = (bf16[1024,512]{1,0:T(8,128)(2,1)S(1)}, bf16[1024,512]{1,0:T(8,128)(2,1)}, u32[]{:S(2)}) copy-start(bf16[1024,512]{1,0:T(8,128)(2,1)} %constant.19.clone.y_inverse) | copy-start | bytes 3145732
  43.2 34.4 %copy-start.4 = (bf16[256,512]{1,0:T(8,128)(2,1)S(1)}, bf16[256,512]{1,0:T(8,128)(2,1)}, u32[]{:S(2)}) copy-start(bf16[256,512]{1,0:T(8,128)(2,1)} %constant.17.clone.time_inverse) | copy-start | bytes 786436
  43.3 34.4 %copy-start.7 = (bf16[256,16]{1,0:T(8,128)(2,1)S(1)}, bf16[256,16]{1,0:T(8,128)(2,1)}, u32[]{:S(2)}) copy-start(bf16[256,16]{1,0:T(8,128)(2,1)} %constant.23.clone.spread) | copy-start | bytes 24580
  43.3 34.4 %copy-start.8 = (bf16[16,16]{1,0:T(8,128)(2,1)S(1)}, bf16[16,16]{1,0:T(8,128)(2,1)}, u32[]{:S(2)}) copy-start(bf16[16,16]{1,0:T(8,128)(2,1)} %bypass.1) | copy-start | bytes 1540

commit v2 on v1

--- a/solution.py
+++ b/solution.py
@@ -364,6 +364,67 @@
         input_grad[0, :, 0, rows] = (mixed + acc[:, rows]).astype(jnp.bfloat16)
 
 
+def exchange_kernel(gx_count, sa_count, packet, landed, send_sem, recv_sem, own_sem):
+    devices = gx_count * sa_count
+    me = lax.axis_index("gx") * sa_count + lax.axis_index("sa")
+
+    def place(other):
+        return (other // sa_count, other % sa_count)
+
+    barrier = pltpu.get_barrier_semaphore()
+
+    @pl.loop(1, devices)
+    def _(step):
+        pl.semaphore_signal(
+            barrier, inc=1, device_id=place((me + step) % devices),
+            device_id_type=pl.DeviceIdType.MESH,
+        )
+
+    own = pltpu.make_async_copy(packet.at[me], landed.at[me], own_sem)
+    own.start()
+    pl.semaphore_wait(barrier, devices - 1)
+
+    def copy(step):
+        other = (me + step) % devices
+        return pltpu.make_async_remote_copy(
+            src_ref=packet.at[other],
+            dst_ref=landed.at[me],
+            send_sem=send_sem.at[step],
+            recv_sem=recv_sem.at[step],
+            device_id=place(other),
+            device_id_type=pl.DeviceIdType.MESH,
+        )
+
+    @pl.loop(1, devices)
+    def _(step):
+        copy(step).start()
+
+    own.wait()
+
+    @pl.loop(1, devices)
+    def _(step):
+        copy(step).wait()
+
+
+def exchange(packet, sizes, collective_id):
+    count = sizes.devices
+    return pl.pallas_call(
+        functools.partial(exchange_kernel, sizes.gx_count, sizes.sa_count),
+        in_specs=[pl.BlockSpec(memory_space=pltpu.VMEM)],
+        out_specs=pl.BlockSpec(memory_space=pltpu.VMEM),
+        out_shape=jax.ShapeDtypeStruct(packet.shape, packet.dtype),
+        scratch_shapes=[
+            pltpu.SemaphoreType.DMA((count,)),
+            pltpu.SemaphoreType.DMA((count,)),
+            pltpu.SemaphoreType.DMA(()),
+        ],
+        compiler_params=pltpu.CompilerParams(
+            collective_id=collective_id, has_side_effects=True
+        ),
+        name="exchange",
+    )(packet)
+
+
 def whole(table):
     return pl.BlockSpec(table.shape, lambda *_: (0,) * table.ndim)
 
@@ -395,7 +456,7 @@
         compiler_params=params,
         name="forward",
     )(inputs, preact, cotangent, time_forward, y_forward)
-    spectra = lax.all_to_all(spectra, ("gx", "sa"), split_axis=0, concat_axis=0, tiled=True)
+    spectra = exchange(spectra, sizes, 0)
     spectra = spectra.reshape((sizes.gx_count, sizes.sa_count) + packet[1:])
     own = sizes.own_pairs
     out_packet = (sizes.gx_count, sizes.sa_count, sizes.groups, sizes.piece, 128)
@@ -426,10 +487,7 @@
         compiler_params=params,
         name="modes",
     )(spectra, mode_weight, x_input, x_grad, x_inverse)
-    grid_rows = lax.all_to_all(
-        grid_rows.reshape((sizes.devices,) + out_packet[2:]),
-        ("gx", "sa"), split_axis=0, concat_axis=0, tiled=True,
-    )
+    grid_rows = exchange(grid_rows.reshape((sizes.devices,) + out_packet[2:]), sizes, 1)
     spread = jnp.asarray(np.repeat(np.eye(channels), 16, axis=0).astype(jnp.bfloat16))
     input_grad = pl.pallas_call(
         functools.partial(inverse_kernel, sizes),

time: 82.7 us -> 88.3 us (1.068)
  the two profiles are of different devices: /device:TPU:0 before, /device:TPU:15 now
where the time goes in v2:
time: 88.3 us; the launch traced here: 87.5 us
  Pallas kernels  77.8 us (88%)
  local copies, waits for them, and re-layouts  8.93 us (10%)
    pallas_call x2, Pallas kernels, exchange(): pl.pallas_call(functools.partial(exchange_kernel, sizes.gx_count, sizes.s...  51 us
    pallas_call x1, Pallas kernels, shards(): pl.pallas_call(functools.partial(mode_kernel, sizes), grid=(channels,), i...  15.4 us
    unnamed x26, local copies, waits for them, and re-layouts  8.93 us
    pallas_call x1, Pallas kernels, shards(): pl.pallas_call(functools.partial(forward_kernel, sizes), grid=(slab,), in...  7.05 us
    pallas_call x1, Pallas kernels, shards(): pl.pallas_call(functools.partial(inverse_kernel, sizes), grid=(slab,), in...  4.4 us

profile of v2, /device:TPU:15, one launch (start us, length us, event | category | flops | bytes accessed | tf_op | source)
XLA Modules:
  0.0 87.5 jit_solution(3806157009410756973)
XLA Ops:
  0.6 0.0 copy-start.4
  0.6 1.2 %copy-done.4 = bf16[512,1024]{1,0:T(8,128)(2,1)S(1)} copy-done((bf16[512,1024]{1,0:T(8,128)(2,1)S(1)}, bf16[512,1024]{1,0:T(8,128)(2,1)}, u32[]{:S(2)}) %copy-start.4) | copy-done | bytes 1048600
  1.9 0.0 copy-start.9
  1.9 0.9 %copy-done.9 = bf16[512,256]{1,0:T(8,128)(2,1)S(1)} copy-done((bf16[512,256]{1,0:T(8,128)(2,1)S(1)}, bf16[512,256]{1,0:T(8,128)(2,1)}, u32[]{:S(2)}) %copy-start.9) | copy-done | bytes 262168
  2.8 7.0 %forward.1 = (bf16[16,4,128,128]{3,2,1,0:T(8,128)(2,1)S(1)}, bf16[32,2,4,16,128]{4,3,2,1,0:T(8,128)(2,1)S(1)}) custom-call(bf16[1,16,4,128,128]{4,3,2,1,0:T(8,128)(2,1)} %inputs.1, bf16[1,16,4,128,128]{4,3,2,1,0:T(8,128)(2,1)} %preact.1, bf16[1,16,4,128,128]{4,3,2,1,0:T(8,128)(2,1)} %cotangent.1, bf16[512,256]{1,0:T(8,128)(2,1)S(1)} %copy-done.9, ...), custom_call_target="tpu_custom_call" | custom-call | tf_op jit(solution)/shard_map/forward/pallas_call | solution.py:446
  9.9 0.0 copy-start.2
  9.9 1.0 %copy-done.2 = bf16[32,2,4,16,128]{4,3,2,1,0:T(8,128)(2,1)} copy-done((bf16[32,2,4,16,128]{4,3,2,1,0:T(8,128)(2,1)}, bf16[32,2,4,16,128]{4,3,2,1,0:T(8,128)(2,1)S(1)}, u32[]{:S(2)}) %copy-start.2) | copy-done | bytes 1048600
  10.8 0.0 copy-start.6
  10.8 31.9 %exchange.2 = bf16[32,2,4,16,128]{4,3,2,1,0:T(8,128)(2,1)} custom-call(bf16[32,2,4,16,128]{4,3,2,1,0:T(8,128)(2,1)} %copy-done.2), custom_call_target="tpu_custom_call" | custom-call | tf_op jit(solution)/shard_map/exchange/pallas_call | solution.py:411
  42.7 0.0 copy-done.6
  42.8 0.0 copy-done.10
  42.8 0.0 copy-start
  42.8 1.2 %copy-done = bf16[32,2,4,16,128]{4,3,2,1,0:T(8,128)(2,1)S(1)} copy-done((bf16[32,2,4,16,128]{4,3,2,1,0:T(8,128)(2,1)S(1)}, bf16[32,2,4,16,128]{4,3,2,1,0:T(8,128)(2,1)}, u32[]{:S(2)}) %copy-start) | copy-done | bytes 1048600
  44.0 0.9 %copy-done.7 = bf16[256,512]{1,0:T(8,128)(2,1)S(1)} copy-done((bf16[256,512]{1,0:T(8,128)(2,1)S(1)}, bf16[256,512]{1,0:T(8,128)(2,1)}, u32[]{:S(2)}) %copy-start.7) | copy-done | bytes 262168
  44.9 15.4 %modes.1 = (f32[16,16,64,128]{3,2,1,0:T(8,128)}, bf16[16,2,4,16,128]{4,3,2,1,0:T(8,128)(2,1)S(1)}) custom-call(bf16[16,2,2,4,16,128]{5,4,3,2,1,0:T(8,128)(2,1)S(1)} %bitcast.2, bf16[16,16,128,128]{3,2,1,0:T(8,128)(2,1)} %weight.1, bf16[256,512]{1,0:T(8,128)(2,1)S(1)} %copy-done.7, bf16[256,512]{1,0:T(8,128)(2,1)S(1)} %copy-done.6, ...), custom_call_target="tpu_custom_call" | custom-call | tf_op jit(solution)/shard_map/modes/pallas_call | solution.py:463
  60.3 0.8 copy-done.5
  61.1 19.1 %exchange.3.grid_rows = bf16[32,4,16,128]{3,2,1,0:T(8,128)(2,1)} custom-call(bf16[32,4,16,128]{3,2,1,0:T(8,128)(2,1)} %bitcast.3), custom_call_target="tpu_custom_call" | custom-call | tf_op jit(solution)/shard_map/exchange/pallas_call | solution.py:411
  80.2 0.0 copy-done.3
  80.2 0.0 copy-done.12
  80.2 0.0 copy-start.1
  80.3 1.0 %copy-done.1 = bf16[32,4,16,128]{3,2,1,0:T(8,128)(2,1)S(1)} copy-done((bf16[32,4,16,128]{3,2,1,0:T(8,128)(2,1)S(1)}, bf16[32,4,16,128]{3,2,1,0:T(8,128)(2,1)}, u32[]{:S(2)}) %copy-start.1) | copy-done | bytes 524312
  81.3 0.9 %copy-done.8 = bf16[256,512]{1,0:T(8,128)(2,1)S(1)} copy-done((bf16[256,512]{1,0:T(8,128)(2,1)S(1)}, bf16[256,512]{1,0:T(8,128)(2,1)}, u32[]{:S(2)}) %copy-start.8) | copy-done | bytes 262168
  82.2 0.8 copy-done.11
  83.1 4.4 %inverse.1 = bf16[1,16,4,128,128]{4,3,2,1,0:T(8,128)(2,1)} custom-call(bf16[32,4,16,128]{3,2,1,0:T(8,128)(2,1)S(1)} %copy-done.1, bf16[16,4,128,128]{3,2,1,0:T(8,128)(2,1)S(1)} %get-tuple-element.8.dz, bf16[16,16]{1,0:T(8,128)(2,1)S(1)} %copy-done.12, bf16[1024,512]{1,0:T(8,128)(2,1)S(1)} %copy-done.3, bf16[256,512]{1,0:T(8,128)(2,1)S(1)} %copy-done.8, ...), custom_call_target="tpu_custom_call" | custom-call | tf_op jit(solution)/shard_map/inverse/pallas_call | solution.py:492
  (7 shorter events, 0.0 us)
Async XLA Ops:
  0.6 1.2 %copy-start.4 = (bf16[512,1024]{1,0:T(8,128)(2,1)S(1)}, bf16[512,1024]{1,0:T(8,128)(2,1)}, u32[]{:S(2)}) copy-start(bf16[512,1024]{1,0:T(8,128)(2,1)} %constant.18.clone.y_forward) | copy-start | bytes 3145732
  1.9 0.9 %copy-start.9 = (bf16[512,256]{1,0:T(8,128)(2,1)S(1)}, bf16[512,256]{1,0:T(8,128)(2,1)}, u32[]{:S(2)}) copy-start(bf16[512,256]{1,0:T(8,128)(2,1)} %constant.16.clone.time_forward) | copy-start | bytes 786436
  9.9 1.0 %copy-start.2 = (bf16[32,2,4,16,128]{4,3,2,1,0:T(8,128)(2,1)}, bf16[32,2,4,16,128]{4,3,2,1,0:T(8,128)(2,1)S(1)}, u32[]{:S(2)}) copy-start(bf16[32,2,4,16,128]{4,3,2,1,0:T(8,128)(2,1)S(1)} %get-tuple-element.6.packet) | copy-start | bytes 3145732
  10.8 31.9 %copy-start.6 = (bf16[256,512]{1,0:T(8,128)(2,1)S(1)}, bf16[256,512]{1,0:T(8,128)(2,1)}, u32[]{:S(2)}) copy-start(bf16[256,512]{1,0:T(8,128)(2,1)} %constant.21.clone.x_grad) | copy-start | bytes 786436
  10.8 31.9 %copy-start.10 = (bf16[256,256]{1,0:T(8,128)(2,1)S(1)}, bf16[256,256]{1,0:T(8,128)(2,1)}, u32[]{:S(2)}) copy-start(bf16[256,256]{1,0:T(8,128)(2,1)} %constant.22.clone.x_inverse) | copy-start | bytes 393220
  42.8 1.2 %copy-start = (bf16[32,2,4,16,128]{4,3,2,1,0:T(8,128)(2,1)S(1)}, bf16[32,2,4,16,128]{4,3,2,1,0:T(8,128)(2,1)}, u32[]{:S(2)}) copy-start(bf16[32,2,4,16,128]{4,3,2,1,0:T(8,128)(2,1)} %exchange.2) | copy-start | bytes 3145732
  44.0 0.9 %copy-start.7 = (bf16[256,512]{1,0:T(8,128)(2,1)S(1)}, bf16[256,512]{1,0:T(8,128)(2,1)}, u32[]{:S(2)}) copy-start(bf16[256,512]{1,0:T(8,128)(2,1)} %constant.20.clone.x_input) | copy-start | bytes 786436
  44.9 35.3 %copy-start.3 = (bf16[1024,512]{1,0:T(8,128)(2,1)S(1)}, bf16[1024,512]{1,0:T(8,128)(2,1)}, u32[]{:S(2)}) copy-start(bf16[1024,512]{1,0:T(8,128)(2,1)} %constant.19.clone.y_inverse) | copy-start | bytes 3145732
  44.9 35.3 %copy-start.12 = (bf16[16,16]{1,0:T(8,128)(2,1)S(1)}, bf16[16,16]{1,0:T(8,128)(2,1)}, u32[]{:S(2)}) copy-start(bf16[16,16]{1,0:T(8,128)(2,1)} %bypass.1) | copy-start | bytes 1540
  60.3 0.8 copy-start.5
  80.2 1.0 %copy-start.1 = (bf16[32,4,16,128]{3,2,1,0:T(8,128)(2,1)S(1)}, bf16[32,4,16,128]{3,2,1,0:T(8,128)(2,1)}, u32[]{:S(2)}) copy-start(bf16[32,4,16,128]{3,2,1,0:T(8,128)(2,1)} %exchange.3.grid_rows) | copy-start | bytes 1572868
  81.3 0.9 %copy-start.8 = (bf16[256,512]{1,0:T(8,128)(2,1)S(1)}, bf16[256,512]{1,0:T(8,128)(2,1)}, u32[]{:S(2)}) copy-start(bf16[256,512]{1,0:T(8,128)(2,1)} %constant.17.clone.time_inverse) | copy-start | bytes 786436
  82.2 0.8 copy-start.11

commit v3 on v1

--- a/solution.py
+++ b/solution.py
@@ -11,6 +11,7 @@
 
 MY = 64
 MT = 32
+VMEM_BYTES = 60 * 2**20
 
 
 root_half = math.sqrt(0.5)
@@ -150,7 +151,6 @@
     cy, sy = host_tables(sizes.modes_y, sizes.cells_y, True)
     cx, sx = host_tables(sizes.modes_x, sizes.cells_x, True)
     group = np.eye(sizes.group, dtype=np.float32)
-    slab = np.eye(sizes.slab, dtype=np.float32)
     rows = np.eye(sizes.rows, dtype=np.float32)
     time = np.stack([ct, -st])
     time_forward = np.einsum("cd,qkt->ctqdk", group, time)
@@ -158,8 +158,8 @@
     time_inverse = time_forward.T
     plane = np.stack([np.stack([cy, sy]), np.stack([-sy, cy])])
     plane = plane.reshape(2, 2, sizes.devices, sizes.rows, sizes.cells_y)
-    y_forward = np.einsum("qpdjy,xz->djxqzpy", plane, slab)
-    y_forward = y_forward.reshape(sizes.devices * sizes.piece, -1)
+    plane = np.einsum("qpdjy->djqpy", plane)
+    y_forward = plane.reshape(2 * sizes.modes_y, -1)
     y_inverse = y_forward.T
     x_table = np.stack(
         [np.concatenate([cx, -sx], 0).T, np.concatenate([sx, cx], 0).T], 1
@@ -213,8 +213,15 @@
     return sizes.sa_count == 2 and sizes.channels == 16
 
 
+def spread_rows(sizes, shape, dim):
+    tall = lax.broadcasted_iota(jnp.int32, shape, dim)
+    short = lax.broadcasted_iota(jnp.int32, shape, 1 - dim)
+    meets = tall // (2 * sizes.slab) * 2 + tall % 2 == short
+    return jnp.where(meets, 1.0, 0.0).astype(jnp.bfloat16)
+
+
 def forward_kernel(
-    sizes, inputs, preact, cotangent, time_forward, y_forward, dz, spectra, in_rows, dz_rows
+    sizes, inputs, preact, cotangent, time_forward, y_forward, dz, spectra, in_rows, dz_rows, wide
 ):
     step = pl.program_id(0)
     slope = gelu_slope(preact[0, :, 0].astype(jnp.float32))
@@ -237,10 +244,23 @@
     time_rows(lambda c: inputs[0, c, 0], in_rows)
     time_rows(lambda c: dz[c, 0], dz_rows)
 
+    @pl.when(step == 0)
+    def _():
+        total = sizes.devices * sizes.piece
+        tall = jnp.dot(
+            spread_rows(sizes, (total, 2 * sizes.modes_y), 0), y_forward[...],
+            preferred_element_type=jnp.float32,
+        )
+        cell = lax.broadcasted_iota(jnp.int32, tall.shape, 0) // 2 % sizes.slab
+        for x in range(sizes.slab):
+            wide[:, pl.ds(x * tall.shape[1], tall.shape[1])] = jnp.where(
+                cell == x, tall, 0.0
+            ).astype(jnp.bfloat16)
+
     @pl.when(step == sizes.slab - 1)
     def _():
         for field, held in enumerate((in_rows, dz_rows)):
-            plane = jnp.dot(y_forward[...], held[...], preferred_element_type=jnp.float32)
+            plane = jnp.dot(wide[...], held[...], preferred_element_type=jnp.float32)
             plane = plane.astype(jnp.bfloat16)
             for cg in range(sizes.groups):
                 spectra[:, field, cg] = plane[:, cg * 128 : (cg + 1) * 128].reshape(
@@ -284,14 +304,16 @@
                                 ] = summed[c * kt : (c + 1) * kt, lanes : lanes + 128]
 
     low = lax.broadcasted_iota(jnp.int32, (16, 128), 1) < sizes.modes_x
-    cg, member = step // sizes.group, step % sizes.group
-    for block in range(sizes.own_pairs // 16):
+    for index in range(2 * (sizes.own_pairs // 16)):
+        within, block = index // (sizes.own_pairs // 16), index % (sizes.own_pairs // 16)
+        channel = step * 2 + within
+        cg, member = channel // sizes.group, channel % sizes.group
         rows = pl.ds(block * 16, 16)
-        left = [[hats[part, s, step, rows] for s in range(samples)] for part in range(2)]
+        left = [[hats[part, s, channel, rows] for s in range(samples)] for part in range(2)]
         total = [[None, None] for _ in range(samples)]
         for o in range(sizes.channels):
             right = [[hats[2 + part, s, o, rows] for s in range(samples)] for part in range(2)]
-            value = weight[0, o, rows].astype(jnp.float32)
+            value = weight[within, o, rows].astype(jnp.float32)
             grad = None
             for s in range(samples):
                 for part in range(2):
@@ -300,7 +322,7 @@
                     term = value * right[part][s]
                     held = total[s][part]
                     total[s][part] = term if held is None else held + term
-            mode_grad[0, o, rows] = grad
+            mode_grad[within, o, rows] = grad
         j, k = divmod(block * 16, kt)
         for s in range(samples):
             real, imag = total[s]
@@ -311,7 +333,7 @@
                 low, real, imag
             ).astype(jnp.bfloat16)
 
-    @pl.when(step == sizes.channels - 1)
+    @pl.when(step == sizes.channels // 2 - 1)
     def _():
         for s in range(samples):
             for cg in range(groups):
@@ -335,9 +357,17 @@
         joined = jnp.concatenate(
             [grid_rows[:, cg].reshape(-1, 128) for cg in range(sizes.groups)], axis=1
         )
-        time_rows[...] = jnp.dot(
-            y_inverse[...], joined, preferred_element_type=jnp.float32
-        ).astype(jnp.bfloat16)
+        total = sizes.devices * sizes.piece
+        long = jnp.dot(
+            y_inverse[...], spread_rows(sizes, (2 * sizes.modes_y, total), 1),
+            preferred_element_type=jnp.float32,
+        )
+        cell = lax.broadcasted_iota(jnp.int32, long.shape, 1) // 2 % sizes.slab
+        for x in range(sizes.slab):
+            table = jnp.where(cell == x, long, 0.0).astype(jnp.bfloat16)
+            time_rows[pl.ds(x * 2 * cells_y, 2 * cells_y)] = jnp.dot(
+                table, joined, preferred_element_type=jnp.float32
+            ).astype(jnp.bfloat16)
         tall = jnp.dot(spread[...], bypass[...], preferred_element_type=jnp.float32)
         wide = lax.dot_general(
             tall.astype(jnp.bfloat16), spread[...], (((1,), (1,)), ((), ())),
@@ -364,6 +394,80 @@
         input_grad[0, :, 0, rows] = (mixed + acc[:, rows]).astype(jnp.bfloat16)
 
 
+def exchange_kernel(gx_count, packet, landed, stage, near, send_sem, recv_sem, own_sem):
+    place, core = lax.axis_index("gx"), lax.axis_index("sa")
+    sibling = 1 - core
+    mesh_ids = dict(device_id_type=pl.DeviceIdType.MESH)
+    barrier = pltpu.get_barrier_semaphore()
+    pl.semaphore_signal(barrier, inc=1, device_id=(place, sibling), **mesh_ids)
+
+    @pl.loop(1, gx_count)
+    def _(step):
+        other = (place + step) % gx_count
+        pl.semaphore_signal(barrier, inc=1, device_id=(other, core), **mesh_ids)
+
+    pl.semaphore_wait(barrier, gx_count)
+    across = pltpu.make_async_remote_copy(
+        src_ref=packet.at[:, sibling], dst_ref=stage, send_sem=near.at[0], recv_sem=near.at[1],
+        device_id=(place, sibling), **mesh_ids,
+    )
+    across.start()
+
+    def send(which, step):
+        other = (place + step) % gx_count
+        source = packet.at[other, core] if which == 0 else stage.at[other]
+        return pltpu.make_async_remote_copy(
+            src_ref=source,
+            dst_ref=landed.at[place, core if which == 0 else sibling],
+            send_sem=send_sem.at[which, step],
+            recv_sem=recv_sem.at[which, step],
+            device_id=(other, core),
+            **mesh_ids,
+        )
+
+    @pl.loop(1, gx_count)
+    def _(step):
+        send(0, step).start()
+
+    own = pltpu.make_async_copy(packet.at[place, core], landed.at[place, core], own_sem.at[0])
+    own.start()
+    across.wait()
+
+    @pl.loop(1, gx_count)
+    def _(step):
+        send(1, step).start()
+
+    passed = pltpu.make_async_copy(stage.at[place], landed.at[place, sibling], own_sem.at[1])
+    passed.start()
+    own.wait()
+    passed.wait()
+    for which in range(2):
+
+        @pl.loop(1, gx_count)
+        def _(step):
+            send(which, step).wait()
+
+
+def exchange(packet, sizes, collective_id):
+    return pl.pallas_call(
+        functools.partial(exchange_kernel, sizes.gx_count),
+        in_specs=[pl.BlockSpec(memory_space=pl.ANY)],
+        out_specs=pl.BlockSpec(memory_space=pl.ANY),
+        out_shape=jax.ShapeDtypeStruct(packet.shape, packet.dtype),
+        scratch_shapes=[
+            pltpu.VMEM((sizes.gx_count,) + packet.shape[2:], packet.dtype),
+            pltpu.SemaphoreType.DMA((2,)),
+            pltpu.SemaphoreType.DMA((2, sizes.gx_count)),
+            pltpu.SemaphoreType.DMA((2, sizes.gx_count)),
+            pltpu.SemaphoreType.DMA((2,)),
+        ],
+        compiler_params=pltpu.CompilerParams(
+            collective_id=collective_id, has_side_effects=True, vmem_limit_bytes=VMEM_BYTES
+        ),
+        name="exchange",
+    )(packet)
+
+
 def whole(table):
     return pl.BlockSpec(table.shape, lambda *_: (0,) * table.ndim)
 
@@ -375,7 +479,7 @@
     tables_built = [jnp.asarray(table) for table in block_tables(sizes)]
     time_forward, time_inverse, y_forward, y_inverse, x_input, x_grad, x_inverse = tables_built
     channels, slab, cells_y, cells_time = inputs.shape[1:]
-    params = pltpu.CompilerParams(vmem_limit_bytes=48 * 2**20)
+    params = pltpu.CompilerParams(vmem_limit_bytes=VMEM_BYTES)
     field_block = pl.BlockSpec(
         (1, channels, 1, cells_y, cells_time), lambda x: (0, 0, x, 0, 0)
     )
@@ -391,28 +495,30 @@
             jax.ShapeDtypeStruct(inputs.shape[1:], jnp.bfloat16),
             jax.ShapeDtypeStruct(packet, jnp.bfloat16),
         ],
-        scratch_shapes=[pltpu.VMEM(rows_shape, jnp.bfloat16)] * 2,
+        scratch_shapes=[pltpu.VMEM(rows_shape, jnp.bfloat16)] * 2
+        + [pltpu.VMEM((sizes.devices * sizes.piece, rows_shape[0]), jnp.bfloat16)],
         compiler_params=params,
         name="forward",
     )(inputs, preact, cotangent, time_forward, y_forward)
-    spectra = lax.all_to_all(spectra, ("gx", "sa"), split_axis=0, concat_axis=0, tiled=True)
-    spectra = spectra.reshape((sizes.gx_count, sizes.sa_count) + packet[1:])
+    spectra = exchange(
+        spectra.reshape((sizes.gx_count, sizes.sa_count) + packet[1:]), sizes, 0
+    )
     own = sizes.own_pairs
     out_packet = (sizes.gx_count, sizes.sa_count, sizes.groups, sizes.piece, 128)
     mode_grad, grid_rows = pl.pallas_call(
         functools.partial(mode_kernel, sizes),
-        grid=(channels,),
+        grid=(channels // 2,),
         in_specs=[
             whole(spectra),
             pl.BlockSpec(
-                (1, channels, own, 128), lambda i: (i, 0, lax.axis_index("sa"), 0)
+                (2, channels, own, 128), lambda i: (i, 0, lax.axis_index("sa"), 0)
             ),
             whole(x_input),
             whole(x_grad),
             whole(x_inverse),
         ],
         out_specs=[
-            pl.BlockSpec((1, channels, own, 128), lambda i: (i, 0, 0, 0)),
+            pl.BlockSpec((2, channels, own, 128), lambda i: (i, 0, 0, 0)),
             pl.BlockSpec(out_packet, lambda i: (0,) * 5),
         ],
         out_shape=[
@@ -426,10 +532,8 @@
         compiler_params=params,
         name="modes",
     )(spectra, mode_weight, x_input, x_grad, x_inverse)
-    grid_rows = lax.all_to_all(
-        grid_rows.reshape((sizes.devices,) + out_packet[2:]),
-        ("gx", "sa"), split_axis=0, concat_axis=0, tiled=True,
-    )
+    grid_rows = exchange(grid_rows, sizes, 1)
+    grid_rows = grid_rows.reshape((sizes.devices,) + out_packet[2:])
     spread = jnp.asarray(np.repeat(np.eye(channels), 16, axis=0).astype(jnp.bfloat16))
     input_grad = pl.pallas_call(
         functools.partial(inverse_kernel, sizes),

time: 82.7 us -> 75.4 us (0.912)
  blocking collectives: 52.3 us -> 0 us
  Pallas kernels: 26.9 us -> 74.3 us
  local copies, waits for them, and re-layouts: 2.22 us -> 0 us
    all_to_all x2 -> x0, blocking collectives: 52.3 us -> none  [the longest x1 33.3 us: shards(): lax.all_to_all(spectra, ('gx', 'sa'), split_axis=0, concat_axis=0, tiled=...]
    pallas_call x1 -> x3, Pallas kernels: 15.4 us -> 59.3 us  [the longest x2 46.8 us: exchange(): pl.pallas_call(functools.partial(exchange_kernel, sizes.gx_count), in_spe...]
    unnamed x18 -> x0, local copies, waits for them, and re-layouts: 2.22 us -> none
    pallas_call x1, Pallas kernels: 4.41 us -> 6.23 us  [shards(): pl.pallas_call(functools.partial(inverse_kernel, sizes), grid=(slab,), in...]
    pallas_call x1, Pallas kernels: 7.05 us -> 8.7 us  [shards(): pl.pallas_call(functools.partial(forward_kernel, sizes), grid=(slab,), in...]
where the time goes in v3:
time: 75.4 us; the launch traced here: 74.9 us
  Pallas kernels  74.3 us (99%)
    pallas_call x2, Pallas kernels, exchange(): pl.pallas_call(functools.partial(exchange_kernel, sizes.gx_count), in_spe...  46.8 us
    pallas_call x1, Pallas kernels, shards(): pl.pallas_call(functools.partial(mode_kernel, sizes), grid=(channels // 2...  12.6 us
    pallas_call x1, Pallas kernels, shards(): pl.pallas_call(functools.partial(forward_kernel, sizes), grid=(slab,), in...  8.7 us
    pallas_call x1, Pallas kernels, shards(): pl.pallas_call(functools.partial(inverse_kernel, sizes), grid=(slab,), in...  6.23 us

profile of v3, /device:TPU:0, one launch (start us, length us, event | category | flops | bytes accessed | tf_op | source)
XLA Modules:
  0.0 74.9 jit_solution(15574522352539788999)
XLA Ops:
  0.6 8.7 %forward.1 = (bf16[16,4,128,128]{3,2,1,0:T(8,128)(2,1)}, bf16[32,2,4,16,128]{4,3,2,1,0:T(8,128)(2,1)}) custom-call(bf16[1,16,4,128,128]{4,3,2,1,0:T(8,128)(2,1)} %inputs.1, bf16[1,16,4,128,128]{4,3,2,1,0:T(8,128)(2,1)} %preact.1, bf16[1,16,4,128,128]{4,3,2,1,0:T(8,128)(2,1)} %cotangent.1, bf16[512,256]{1,0:T(8,128)(2,1)} %constant.16.clone.time_forward, ...), custom_call_target="tpu_custom_call" | custom-call | tf_op jit(solution)/shard_map/forward/pallas_call | solution.py:489
  9.3 27.1 %exchange.2.spectra = bf16[16,2,2,4,16,128]{5,4,3,2,1,0:T(8,128)(2,1)} custom-call(bf16[16,2,2,4,16,128]{5,4,3,2,1,0:T(8,128)(2,1)} %bitcast.3), custom_call_target="tpu_custom_call" | custom-call | tf_op jit(solution)/shard_map/exchange/pallas_call | solution.py:452
  36.4 12.6 %modes.1 = (f32[16,16,64,128]{3,2,1,0:T(8,128)}, bf16[16,2,4,16,128]{4,3,2,1,0:T(8,128)(2,1)}) custom-call(bf16[16,2,2,4,16,128]{5,4,3,2,1,0:T(8,128)(2,1)} %exchange.2.spectra, bf16[16,16,128,128]{3,2,1,0:T(8,128)(2,1)} %weight.1, bf16[256,512]{1,0:T(8,128)(2,1)} %constant.20.clone.x_input, bf16[256,512]{1,0:T(8,128)(2,1)} %constant.21.clone.x_grad, ...), custom_call_target="tpu_custom_call" | custom-call | tf_op jit(solution)/shard_map/modes/pallas_call | solution.py:508
  49.0 19.7 %exchange.3 = bf16[16,2,4,16,128]{4,3,2,1,0:T(8,128)(2,1)} custom-call(bf16[16,2,4,16,128]{4,3,2,1,0:T(8,128)(2,1)} %get-tuple-element.7.packet), custom_call_target="tpu_custom_call" | custom-call | tf_op jit(solution)/shard_map/exchange/pallas_call | solution.py:452
  68.7 6.2 %inverse.1 = bf16[1,16,4,128,128]{4,3,2,1,0:T(8,128)(2,1)} custom-call(bf16[32,4,16,128]{3,2,1,0:T(8,128)(2,1)} %bitcast.2, bf16[16,4,128,128]{3,2,1,0:T(8,128)(2,1)} %get-tuple-element.8.dz, bf16[16,16]{1,0:T(8,128)(2,1)} %bypass.1, bf16[256,128]{1,0:T(8,128)(2,1)} %constant.19.clone.y_inverse, bf16[256,512]{1,0:T(8,128)(2,1)} %constant.17.clone.time_inverse, ...), custom_call_target="tpu_custom_call" | custom-call | tf_op jit(solution)/shard_map/inverse/pallas_call | solution.py:538

commit v4 on v3

--- a/solution.py
+++ b/solution.py
@@ -394,78 +394,37 @@
         input_grad[0, :, 0, rows] = (mixed + acc[:, rows]).astype(jnp.bfloat16)
 
 
-def exchange_kernel(gx_count, packet, landed, stage, near, send_sem, recv_sem, own_sem):
+def sibling_kernel(packet, landed, near, own_sem):
     place, core = lax.axis_index("gx"), lax.axis_index("sa")
     sibling = 1 - core
-    mesh_ids = dict(device_id_type=pl.DeviceIdType.MESH)
+    own = pltpu.make_async_copy(packet.at[:, core], landed.at[:, core], own_sem)
+    own.start()
+    mesh_ids = dict(device_id=(place, sibling), device_id_type=pl.DeviceIdType.MESH)
     barrier = pltpu.get_barrier_semaphore()
-    pl.semaphore_signal(barrier, inc=1, device_id=(place, sibling), **mesh_ids)
-
-    @pl.loop(1, gx_count)
-    def _(step):
-        other = (place + step) % gx_count
-        pl.semaphore_signal(barrier, inc=1, device_id=(other, core), **mesh_ids)
-
-    pl.semaphore_wait(barrier, gx_count)
+    pl.semaphore_signal(barrier, inc=1, **mesh_ids)
+    pl.semaphore_wait(barrier, 1)
     across = pltpu.make_async_remote_copy(
-        src_ref=packet.at[:, sibling], dst_ref=stage, send_sem=near.at[0], recv_sem=near.at[1],
-        device_id=(place, sibling), **mesh_ids,
+        src_ref=packet.at[:, sibling], dst_ref=landed.at[:, core],
+        send_sem=near.at[0], recv_sem=near.at[1], **mesh_ids,
     )
     across.start()
-
-    def send(which, step):
-        other = (place + step) % gx_count
-        source = packet.at[other, core] if which == 0 else stage.at[other]
-        return pltpu.make_async_remote_copy(
-            src_ref=source,
-            dst_ref=landed.at[place, core if which == 0 else sibling],
-            send_sem=send_sem.at[which, step],
-            recv_sem=recv_sem.at[which, step],
-            device_id=(other, core),
-            **mesh_ids,
-        )
-
-    @pl.loop(1, gx_count)
-    def _(step):
-        send(0, step).start()
-
-    own = pltpu.make_async_copy(packet.at[place, core], landed.at[place, core], own_sem.at[0])
-    own.start()
+    own.wait()
     across.wait()
 
-    @pl.loop(1, gx_count)
-    def _(step):
-        send(1, step).start()
-
-    passed = pltpu.make_async_copy(stage.at[place], landed.at[place, sibling], own_sem.at[1])
-    passed.start()
-    own.wait()
-    passed.wait()
-    for which in range(2):
-
-        @pl.loop(1, gx_count)
-        def _(step):
-            send(which, step).wait()
-
-
-def exchange(packet, sizes, collective_id):
-    return pl.pallas_call(
-        functools.partial(exchange_kernel, sizes.gx_count),
+
+def exchange(packet, collective_id):
+    swapped = pl.pallas_call(
+        sibling_kernel,
         in_specs=[pl.BlockSpec(memory_space=pl.ANY)],
         out_specs=pl.BlockSpec(memory_space=pl.ANY),
         out_shape=jax.ShapeDtypeStruct(packet.shape, packet.dtype),
-        scratch_shapes=[
-            pltpu.VMEM((sizes.gx_count,) + packet.shape[2:], packet.dtype),
-            pltpu.SemaphoreType.DMA((2,)),
-            pltpu.SemaphoreType.DMA((2, sizes.gx_count)),
-            pltpu.SemaphoreType.DMA((2, sizes.gx_count)),
-            pltpu.SemaphoreType.DMA((2,)),
-        ],
+        scratch_shapes=[pltpu.SemaphoreType.DMA((2,)), pltpu.SemaphoreType.DMA(())],
         compiler_params=pltpu.CompilerParams(
             collective_id=collective_id, has_side_effects=True, vmem_limit_bytes=VMEM_BYTES
         ),
-        name="exchange",
+        name="sibling",
     )(packet)
+    return lax.all_to_all(swapped, "gx", split_axis=0, concat_axis=0, tiled=True)
 
 
 def whole(table):
@@ -500,9 +459,7 @@
         compiler_params=params,
         name="forward",
     )(inputs, preact, cotangent, time_forward, y_forward)
-    spectra = exchange(
-        spectra.reshape((sizes.gx_count, sizes.sa_count) + packet[1:]), sizes, 0
-    )
+    spectra = exchange(spectra.reshape((sizes.gx_count, sizes.sa_count) + packet[1:]), 0)
     own = sizes.own_pairs
     out_packet = (sizes.gx_count, sizes.sa_count, sizes.groups, sizes.piece, 128)
     mode_grad, grid_rows = pl.pallas_call(
@@ -532,7 +489,7 @@
         compiler_params=params,
         name="modes",
     )(spectra, mode_weight, x_input, x_grad, x_inverse)
-    grid_rows = exchange(grid_rows, sizes, 1)
+    grid_rows = exchange(grid_rows, 1)
     grid_rows = grid_rows.reshape((sizes.devices,) + out_packet[2:])
     spread = jnp.asarray(np.repeat(np.eye(channels), 16, axis=0).astype(jnp.bfloat16))
     input_grad = pl.pallas_call(

time: 75.4 us -> 108 us (1.43)
  blocking collectives: 0 us -> 53.2 us
  Pallas kernels: 74.3 us -> 53.5 us
    all_to_all x0 -> x2, blocking collectives: none -> 53.2 us  [exchange(): lax.all_to_all(swapped, 'gx', split_axis=0, concat_axis=0, tiled=True)]
    pallas_call x2, Pallas kernels: 46.8 us -> 26.1 us  [exchange(): pl.pallas_call(sibling_kernel, in_specs=[pl.BlockSpec(memory_space=pl.ANY...]
where the time goes in v4:
time: 108 us; the launch traced here: 107 us
  Pallas kernels  53.5 us (50%)
  blocking collectives  53.2 us (49%)
    all_to_all x2, blocking collectives, exchange(): lax.all_to_all(swapped, 'gx', split_axis=0, concat_axis=0, tiled=True)  53.2 us
    pallas_call x2, Pallas kernels, exchange(): pl.pallas_call(sibling_kernel, in_specs=[pl.BlockSpec(memory_space=pl.ANY...  26.1 us
    pallas_call x1, Pallas kernels, shards(): pl.pallas_call(functools.partial(mode_kernel, sizes), grid=(channels // 2...  12.5 us
    pallas_call x1, Pallas kernels, shards(): pl.pallas_call(functools.partial(forward_kernel, sizes), grid=(slab,), in...  8.7 us
    pallas_call x1, Pallas kernels, shards(): pl.pallas_call(functools.partial(inverse_kernel, sizes), grid=(slab,), in...  6.21 us

profile of v4, /device:TPU:0, one launch (start us, length us, event | category | flops | bytes accessed | tf_op | source)
XLA Modules:
  0.0 107.4 jit_solution(4494657998879199556)
XLA Ops:
  0.6 8.7 %forward.1 = (bf16[16,4,128,128]{3,2,1,0:T(8,128)(2,1)}, bf16[32,2,4,16,128]{4,3,2,1,0:T(8,128)(2,1)}) custom-call(bf16[1,16,4,128,128]{4,3,2,1,0:T(8,128)(2,1)} %inputs.1, bf16[1,16,4,128,128]{4,3,2,1,0:T(8,128)(2,1)} %preact.1, bf16[1,16,4,128,128]{4,3,2,1,0:T(8,128)(2,1)} %cotangent.1, bf16[512,256]{1,0:T(8,128)(2,1)} %constant.16.clone.time_forward, ...), custom_call_target="tpu_custom_call" | custom-call | tf_op jit(solution)/shard_map/forward/pallas_call | solution.py:448
  9.3 17.0 %sibling.2 = bf16[16,2,2,4,16,128]{5,4,3,2,1,0:T(8,128)(2,1)} custom-call(bf16[16,2,2,4,16,128]{5,4,3,2,1,0:T(8,128)(2,1)} %bitcast.3), custom_call_target="tpu_custom_call" | custom-call | tf_op jit(solution)/shard_map/sibling/pallas_call | solution.py:416
  26.4 34.8 %all_to_all.10.spectra = bf16[16,2,2,4,16,128]{5,4,3,2,1,0:T(8,128)(2,1)} all-to-all(bf16[16,2,2,4,16,128]{5,4,3,2,1,0:T(8,128)(2,1)} %sibling.2), channel_id=1, replica_groups=mesh['gx'=16,'sa'=2] {'gx'}, dimensions={0} | all-to-all | bytes 2097152 | tf_op jit(solution)/shard_map/all_to_all | solution.py:427
  61.2 12.5 %modes.1 = (f32[16,16,64,128]{3,2,1,0:T(8,128)}, bf16[16,2,4,16,128]{4,3,2,1,0:T(8,128)(2,1)}) custom-call(bf16[16,2,2,4,16,128]{5,4,3,2,1,0:T(8,128)(2,1)} %all_to_all.10.spectra, bf16[16,16,128,128]{3,2,1,0:T(8,128)(2,1)} %weight.1, bf16[256,512]{1,0:T(8,128)(2,1)} %constant.20.clone.x_input, bf16[256,512]{1,0:T(8,128)(2,1)} %constant.21.clone.x_grad, ...), custom_call_target="tpu_custom_call" | custom-call | tf_op jit(solution)/shard_map/modes/pallas_call | solution.py:465
  73.7 9.1 %sibling.3 = bf16[16,2,4,16,128]{4,3,2,1,0:T(8,128)(2,1)} custom-call(bf16[16,2,4,16,128]{4,3,2,1,0:T(8,128)(2,1)} %get-tuple-element.7.packet), custom_call_target="tpu_custom_call" | custom-call | tf_op jit(solution)/shard_map/sibling/pallas_call | solution.py:416
  82.8 18.4 %all_to_all.11 = bf16[16,2,4,16,128]{4,3,2,1,0:T(8,128)(2,1)} all-to-all(bf16[16,2,4,16,128]{4,3,2,1,0:T(8,128)(2,1)} %sibling.3), channel_id=1, replica_groups=mesh['gx'=16,'sa'=2] {'gx'}, dimensions={0} | all-to-all | bytes 1048576 | tf_op jit(solution)/shard_map/all_to_all | solution.py:427
  101.2 6.2 %inverse.1 = bf16[1,16,4,128,128]{4,3,2,1,0:T(8,128)(2,1)} custom-call(bf16[32,4,16,128]{3,2,1,0:T(8,128)(2,1)} %bitcast.2, bf16[16,4,128,128]{3,2,1,0:T(8,128)(2,1)} %get-tuple-element.8.dz, bf16[16,16]{1,0:T(8,128)(2,1)} %bypass.1, bf16[256,128]{1,0:T(8,128)(2,1)} %constant.19.clone.y_inverse, bf16[256,512]{1,0:T(8,128)(2,1)} %constant.17.clone.time_inverse, ...), custom_call_target="tpu_custom_call" | custom-call | tf_op jit(solution)/shard_map/inverse/pallas_call | solution.py:495

commit v5 on v3

--- a/solution.py
+++ b/solution.py
@@ -263,7 +263,8 @@
             plane = jnp.dot(wide[...], held[...], preferred_element_type=jnp.float32)
             plane = plane.astype(jnp.bfloat16)
             for cg in range(sizes.groups):
-                spectra[:, field, cg] = plane[:, cg * 128 : (cg + 1) * 128].reshape(
+                rows = pl.ds((field * sizes.groups + cg) * sizes.piece, sizes.piece)
+                spectra[:, rows] = plane[:, cg * 128 : (cg + 1) * 128].reshape(
                     sizes.devices, sizes.piece, 128
                 )
 
@@ -289,7 +290,8 @@
         ):
             for s in range(samples):
                 for cg in range(groups):
-                    block = spectra[:, s, field, cg].reshape(-1, 128)
+                    first = (field * groups + cg) * sizes.piece
+                    block = spectra[:, s, pl.ds(first, sizes.piece)].reshape(-1, 128)
                     summed = lax.dot_general(
                         block, table[...], (((0,), (0,)), ((), ())),
                         preferred_element_type=jnp.float32,
@@ -341,7 +343,8 @@
                     x_inverse[...], back[s, cg], (((1,), (1,)), ((), ())),
                     preferred_element_type=jnp.float32,
                 )
-                rows_out[:, s, cg] = grid_rows.astype(jnp.bfloat16).reshape(
+                rows = pl.ds(cg * sizes.piece, sizes.piece)
+                rows_out[:, s, rows] = grid_rows.astype(jnp.bfloat16).reshape(
                     sizes.gx_count, sizes.piece, 128
                 )
 
@@ -355,7 +358,11 @@
     @pl.when(step == 0)
     def _():
         joined = jnp.concatenate(
-            [grid_rows[:, cg].reshape(-1, 128) for cg in range(sizes.groups)], axis=1
+            [
+                grid_rows[:, pl.ds(cg * sizes.piece, sizes.piece)].reshape(-1, 128)
+                for cg in range(sizes.groups)
+            ],
+            axis=1,
         )
         total = sizes.devices * sizes.piece
         long = jnp.dot(
@@ -484,13 +491,13 @@
         (1, channels, 1, cells_y, cells_time), lambda x: (0, 0, x, 0, 0)
     )
     dz_block = pl.BlockSpec((channels, 1, cells_y, cells_time), lambda x: (0, x, 0, 0))
-    packet = (sizes.devices, 2, sizes.groups, sizes.piece, 128)
+    packet = (sizes.devices, 2 * sizes.groups * sizes.piece, 128)
     rows_shape = (2 * slab * cells_y, sizes.groups * 128)
     dz, spectra = pl.pallas_call(
         functools.partial(forward_kernel, sizes),
         grid=(slab,),
         in_specs=[field_block] * 3 + [whole(time_forward), whole(y_forward)],
-        out_specs=[dz_block, pl.BlockSpec(packet, lambda x: (0,) * 5)],
+        out_specs=[dz_block, pl.BlockSpec(packet, lambda x: (0,) * 3)],
         out_shape=[
             jax.ShapeDtypeStruct(inputs.shape[1:], jnp.bfloat16),
             jax.ShapeDtypeStruct(packet, jnp.bfloat16),
@@ -504,7 +511,7 @@
         spectra.reshape((sizes.gx_count, sizes.sa_count) + packet[1:]), sizes, 0
     )
     own = sizes.own_pairs
-    out_packet = (sizes.gx_count, sizes.sa_count, sizes.groups, sizes.piece, 128)
+    out_packet = (sizes.gx_count, sizes.sa_count, sizes.groups * sizes.piece, 128)
     mode_grad, grid_rows = pl.pallas_call(
         functools.partial(mode_kernel, sizes),
         grid=(channels // 2,),
@@ -519,7 +526,7 @@
         ],
         out_specs=[
             pl.BlockSpec((2, channels, own, 128), lambda i: (i, 0, 0, 0)),
-            pl.BlockSpec(out_packet, lambda i: (0,) * 5),
+            pl.BlockSpec(out_packet, lambda i: (0,) * 4),
         ],
         out_shape=[
             jax.ShapeDtypeStruct((channels, channels, own, 128), jnp.float32),

time: 75.4 us -> 75.4 us (level)
  no operation moved by 1% of the time
where the time goes in v5:
time: 75.4 us; the launch traced here: 74.9 us
  Pallas kernels  74.3 us (99%)
    pallas_call x2, Pallas kernels, exchange(): pl.pallas_call(functools.partial(exchange_kernel, sizes.gx_count), in_spe...  46.8 us
    pallas_call x1, Pallas kernels, shards(): pl.pallas_call(functools.partial(mode_kernel, sizes), grid=(channels // 2...  12.6 us
    pallas_call x1, Pallas kernels, shards(): pl.pallas_call(functools.partial(forward_kernel, sizes), grid=(slab,), in...  8.7 us
    pallas_call x1, Pallas kernels, shards(): pl.pallas_call(functools.partial(inverse_kernel, sizes), grid=(slab,), in...  6.23 us

profile of v5, /device:TPU:0, one launch (start us, length us, event | category | flops | bytes accessed | tf_op | source)
XLA Modules:
  0.0 74.9 jit_solution(15574522352539788999)
XLA Ops:
  0.6 8.7 %forward.1 = (bf16[16,4,128,128]{3,2,1,0:T(8,128)(2,1)}, bf16[32,128,128]{2,1,0:T(8,128)(2,1)}) custom-call(bf16[1,16,4,128,128]{4,3,2,1,0:T(8,128)(2,1)} %inputs.1, bf16[1,16,4,128,128]{4,3,2,1,0:T(8,128)(2,1)} %preact.1, bf16[1,16,4,128,128]{4,3,2,1,0:T(8,128)(2,1)} %cotangent.1, bf16[512,256]{1,0:T(8,128)(2,1)} %constant.16.clone.time_forward, ...), custom_call_target="tpu_custom_call" | custom-call | tf_op jit(solution)/shard_map/forward/pallas_call | solution.py:496
  9.3 27.1 %exchange.2.spectra = bf16[16,2,128,128]{3,2,1,0:T(8,128)(2,1)} custom-call(bf16[16,2,128,128]{3,2,1,0:T(8,128)(2,1)} %bitcast.3), custom_call_target="tpu_custom_call" | custom-call | tf_op jit(solution)/shard_map/exchange/pallas_call | solution.py:459
  36.4 12.6 %modes.1 = (f32[16,16,64,128]{3,2,1,0:T(8,128)}, bf16[16,2,64,128]{3,2,1,0:T(8,128)(2,1)}) custom-call(bf16[16,2,128,128]{3,2,1,0:T(8,128)(2,1)} %exchange.2.spectra, bf16[16,16,128,128]{3,2,1,0:T(8,128)(2,1)} %weight.1, bf16[256,512]{1,0:T(8,128)(2,1)} %constant.20.clone.x_input, bf16[256,512]{1,0:T(8,128)(2,1)} %constant.21.clone.x_grad, ...), custom_call_target="tpu_custom_call" | custom-call | tf_op jit(solution)/shard_map/modes/pallas_call | solution.py:515
  49.0 19.7 %exchange.3 = bf16[16,2,64,128]{3,2,1,0:T(8,128)(2,1)} custom-call(bf16[16,2,64,128]{3,2,1,0:T(8,128)(2,1)} %get-tuple-element.7.packet), custom_call_target="tpu_custom_call" | custom-call | tf_op jit(solution)/shard_map/exchange/pallas_call | solution.py:459
  68.7 6.2 %inverse.1 = bf16[1,16,4,128,128]{4,3,2,1,0:T(8,128)(2,1)} custom-call(bf16[32,64,128]{2,1,0:T(8,128)(2,1)} %bitcast.2, bf16[16,4,128,128]{3,2,1,0:T(8,128)(2,1)} %get-tuple-element.8.dz, bf16[16,16]{1,0:T(8,128)(2,1)} %bypass.1, bf16[256,128]{1,0:T(8,128)(2,1)} %constant.19.clone.y_inverse, bf16[256,512]{1,0:T(8,128)(2,1)} %constant.17.clone.time_inverse, ...), custom_call_target="tpu_custom_call" | custom-call | tf_op jit(solution)/shard_map/inverse/pallas_call | solution.py:545

commit v6 on v5

--- a/solution.py
+++ b/solution.py
@@ -306,9 +306,9 @@
                                 ] = summed[c * kt : (c + 1) * kt, lanes : lanes + 128]
 
     low = lax.broadcasted_iota(jnp.int32, (16, 128), 1) < sizes.modes_x
-    for index in range(2 * (sizes.own_pairs // 16)):
+    for index in range(4 * (sizes.own_pairs // 16)):
         within, block = index // (sizes.own_pairs // 16), index % (sizes.own_pairs // 16)
-        channel = step * 2 + within
+        channel = step * 4 + within
         cg, member = channel // sizes.group, channel % sizes.group
         rows = pl.ds(block * 16, 16)
         left = [[hats[part, s, channel, rows] for s in range(samples)] for part in range(2)]
@@ -335,7 +335,7 @@
                 low, real, imag
             ).astype(jnp.bfloat16)
 
-    @pl.when(step == sizes.channels // 2 - 1)
+    @pl.when(step == sizes.channels // 4 - 1)
     def _():
         for s in range(samples):
             for cg in range(groups):
@@ -458,8 +458,8 @@
 def exchange(packet, sizes, collective_id):
     return pl.pallas_call(
         functools.partial(exchange_kernel, sizes.gx_count),
-        in_specs=[pl.BlockSpec(memory_space=pl.ANY)],
-        out_specs=pl.BlockSpec(memory_space=pl.ANY),
+        in_specs=[pl.BlockSpec(memory_space=pltpu.VMEM)],
+        out_specs=pl.BlockSpec(memory_space=pltpu.VMEM),
         out_shape=jax.ShapeDtypeStruct(packet.shape, packet.dtype),
         scratch_shapes=[
             pltpu.VMEM((sizes.gx_count,) + packet.shape[2:], packet.dtype),
@@ -514,18 +514,18 @@
     out_packet = (sizes.gx_count, sizes.sa_count, sizes.groups * sizes.piece, 128)
     mode_grad, grid_rows = pl.pallas_call(
         functools.partial(mode_kernel, sizes),
-        grid=(channels // 2,),
+        grid=(channels // 4,),
         in_specs=[
             whole(spectra),
             pl.BlockSpec(
-                (2, channels, own, 128), lambda i: (i, 0, lax.axis_index("sa"), 0)
+                (4, channels, own, 128), lambda i: (i, 0, lax.axis_index("sa"), 0)
             ),
             whole(x_input),
             whole(x_grad),
             whole(x_inverse),
         ],
         out_specs=[
-            pl.BlockSpec((2, channels, own, 128), lambda i: (i, 0, 0, 0)),
+            pl.BlockSpec((4, channels, own, 128), lambda i: (i, 0, 0, 0)),
             pl.BlockSpec(out_packet, lambda i: (0,) * 4),
         ],
         out_shape=[

time: 75.4 us -> 77.6 us (1.029)
  Pallas kernels: 74.3 us -> 76.5 us
    pallas_call x2, Pallas kernels: 46.8 us -> 50.2 us  [exchange(): pl.pallas_call(functools.partial(exchange_kernel, sizes.gx_count), in_spe...]
    pallas_call x1, Pallas kernels: 12.6 us -> 11.4 us  [shards(): pl.pallas_call(functools.partial(mode_kernel, sizes), grid=(channels // 4...]
where the time goes in v6:
time: 77.6 us; the launch traced here: 77.1 us
  Pallas kernels  76.5 us (99%)
    pallas_call x2, Pallas kernels, exchange(): pl.pallas_call(functools.partial(exchange_kernel, sizes.gx_count), in_spe...  50.2 us
    pallas_call x1, Pallas kernels, shards(): pl.pallas_call(functools.partial(mode_kernel, sizes), grid=(channels // 4...  11.4 us
    pallas_call x1, Pallas kernels, shards(): pl.pallas_call(functools.partial(forward_kernel, sizes), grid=(slab,), in...  8.7 us
    pallas_call x1, Pallas kernels, shards(): pl.pallas_call(functools.partial(inverse_kernel, sizes), grid=(slab,), in...  6.24 us

profile of v6, /device:TPU:0, one launch (start us, length us, event | category | flops | bytes accessed | tf_op | source)
XLA Modules:
  0.0 77.1 jit_solution(6244032812016906136)
XLA Ops:
  0.6 8.7 %forward.1 = (bf16[16,4,128,128]{3,2,1,0:T(8,128)(2,1)}, bf16[32,128,128]{2,1,0:T(8,128)(2,1)}) custom-call(bf16[1,16,4,128,128]{4,3,2,1,0:T(8,128)(2,1)} %inputs.1, bf16[1,16,4,128,128]{4,3,2,1,0:T(8,128)(2,1)} %preact.1, bf16[1,16,4,128,128]{4,3,2,1,0:T(8,128)(2,1)} %cotangent.1, bf16[512,256]{1,0:T(8,128)(2,1)} %constant.16.clone.time_forward, ...), custom_call_target="tpu_custom_call" | custom-call | tf_op jit(solution)/shard_map/forward/pallas_call | solution.py:496
  9.3 28.9 %exchange.2.spectra = bf16[16,2,128,128]{3,2,1,0:T(8,128)(2,1)} custom-call(bf16[16,2,128,128]{3,2,1,0:T(8,128)(2,1)} %bitcast.3), custom_call_target="tpu_custom_call" | custom-call | tf_op jit(solution)/shard_map/exchange/pallas_call | solution.py:459
  38.3 11.4 %modes.1 = (f32[16,16,64,128]{3,2,1,0:T(8,128)}, bf16[16,2,64,128]{3,2,1,0:T(8,128)(2,1)}) custom-call(bf16[16,2,128,128]{3,2,1,0:T(8,128)(2,1)} %exchange.2.spectra, bf16[16,16,128,128]{3,2,1,0:T(8,128)(2,1)} %weight.1, bf16[256,512]{1,0:T(8,128)(2,1)} %constant.20.clone.x_input, bf16[256,512]{1,0:T(8,128)(2,1)} %constant.21.clone.x_grad, ...), custom_call_target="tpu_custom_call" | custom-call | tf_op jit(solution)/shard_map/modes/pallas_call | solution.py:515
  49.6 21.2 %exchange.3 = bf16[16,2,64,128]{3,2,1,0:T(8,128)(2,1)} custom-call(bf16[16,2,64,128]{3,2,1,0:T(8,128)(2,1)} %get-tuple-element.7.packet), custom_call_target="tpu_custom_call" | custom-call | tf_op jit(solution)/shard_map/exchange/pallas_call | solution.py:459
  70.9 6.2 %inverse.1 = bf16[1,16,4,128,128]{4,3,2,1,0:T(8,128)(2,1)} custom-call(bf16[32,64,128]{2,1,0:T(8,128)(2,1)} %bitcast.2, bf16[16,4,128,128]{3,2,1,0:T(8,128)(2,1)} %get-tuple-element.8.dz, bf16[16,16]{1,0:T(8,128)(2,1)} %bypass.1, bf16[256,128]{1,0:T(8,128)(2,1)} %constant.19.clone.y_inverse, bf16[256,512]{1,0:T(8,128)(2,1)} %constant.17.clone.time_inverse, ...), custom_call_target="tpu_custom_call" | custom-call | tf_op jit(solution)/shard_map/inverse/pallas_call | solution.py:545
